TPU v7x, 256 devices: a whole 4x4x8 slice. The times are simulated.
256 devices in a mesh: dp: 32 (over x, y, core), tensor: 8 (over z).
Axes of the slice: x: 4, y: 4, z: 8, core: 2. Of those that a mesh axis runs over, the one named last changes fastest.
Arguments:
- tokens: bfloat16 [65536, 5120], P('dp', 'tensor'), may hold values from -6 to 6
- cotangent: bfloat16 [65536, 1024], P('dp', 'tensor'), may hold values from -6 to 6
- base_weight: bfloat16 [5120, 1024], P('tensor'), may hold values from -0.078125 to 0.078125
- adapter_down: float32 [128, 5120, 64], P('dp', 'tensor'), may hold values from -0.078125 to 0.078125
- adapter_up: float32 [128, 64, 1024], P('dp', None, 'tensor'), may hold values from -0.75 to 0.75
- block_adapter: int32 [512], P('dp'), may hold values from 0 to 127, as said below
- adapter_slot: int32 [128], replicated, may hold values from 0 to 127, as said below
- adapter_rank: int32 [128], replicated, may hold values from 16 to 64, as said below
Outputs:
- values: bfloat16 [65536, 1024], P('dp', 'tensor')
- token_input_gradient: bfloat16 [65536, 5120], P('dp', 'tensor')
- down_matrix_gradient: float32 [128, 5120, 64], P('dp', 'tensor')
- up_matrix_gradient: float32 [128, 64, 1024], P('dp', None, 'tensor')
Inputs may be any that keep to these rules, and one draw needn't show every extreme that they name: adapter_slot is a permutation; the owner of slot s is index s // 4 of dp. `block_adapter`: among the 16 blocks of one index of dp, at most 1 name adapters of any one owner; in every draw one owner gets exactly 1 block from every index of dp. `adapter_rank`: each rank is a multiple of 16.
All inputs are finite; a program needn't handle non-finite values.
Results may differ from a plain program's by a relative error of at most 0.02.
Values may be sent and summed in bfloat16 or wider, within the bound.
A program may use at most 128 MiB of HBM per device.

v0:
```python
import jax
import jax.numpy as jnp
from jax import lax
from jax.sharding import PartitionSpec as P


def tally_slots(tags, pieces, per_owner):
    sums = []
    for owned_index in range(per_owner):
        chosen = tags == owned_index + 1
        chosen = chosen.reshape((-1,) + (1,) * (pieces.ndim - 1))
        sums.append(jnp.sum(jnp.where(chosen, pieces, jnp.zeros((), pieces.dtype)), axis=0))
    return jnp.stack(sums)


def on_device(
    tokens,
    cotangent,
    base_weight,
    adapter_down,
    adapter_up,
    block_adapter,
    adapter_slot,
    adapter_rank,
):
    owners = lax.axis_size("dp")
    blocks = block_adapter.shape[0]
    per_owner = adapter_down.shape[0]
    capacity = max(1, blocks // owners)
    slots_all = owners * capacity
    tok_rows, feat_width = tokens.shape
    head_width = cotangent.shape[1]
    block_rows = tok_rows // blocks
    rank_max = adapter_down.shape[2]
    adapters = adapter_slot.shape[0]
    picked = block_adapter[:, None] == jnp.arange(adapters, dtype=jnp.int32)[None, :]
    block_slot = jnp.sum(jnp.where(picked, adapter_slot[None, :], 0), axis=1)
    block_owner = block_slot // per_owner
    block_local = block_slot % per_owner
    earlier = jnp.arange(blocks)[None, :] < jnp.arange(blocks)[:, None]
    same_owner = block_owner[:, None] == block_owner[None, :]
    position = jnp.sum(same_owner & earlier, axis=1)
    target = block_owner * capacity + position
    matched = target[None, :] == jnp.arange(slots_all, dtype=jnp.int32)[:, None]
    filled = jnp.any(matched, axis=1)
    source_block = jnp.argmax(matched.astype(jnp.int32), axis=1)
    request = jnp.where(filled, block_local[source_block] + 1, 0)

    def gather_slots(block_array):
        chosen = filled.reshape((-1,) + (1,) * (block_array.ndim - 1))
        picked_rows = jnp.where(chosen, block_array[source_block], jnp.zeros((), block_array.dtype))
        return picked_rows.reshape((owners, capacity) + block_array.shape[1:])

    token_blocks = tokens.reshape(blocks, block_rows, feat_width)
    grad_blocks = cotangent.reshape(blocks, block_rows, head_width)
    owner_index = lax.axis_index("dp")
    own_slots = owner_index * per_owner + jnp.arange(per_owner, dtype=jnp.int32)
    owned_mask = adapter_slot[None, :] == own_slots[:, None]
    own_rank = jnp.sum(jnp.where(owned_mask, adapter_rank[None, :], 0), axis=1)
    active = (jnp.arange(rank_max)[None, :] < own_rank[:, None]).astype(jnp.float32)
    down_weights = (adapter_down * active[:, None, :]).astype(jnp.bfloat16)
    up_weights = (adapter_up * active[:, :, None]).astype(jnp.bfloat16)
    own_scale = rank_max / (4.0 * own_rank.astype(jnp.float32))
    sent_rows = gather_slots(token_blocks)
    sent_grads = gather_slots(grad_blocks)
    arrived_rows, arrived_grads, arrived_tags = (
        lax.all_to_all(sent_rows, "dp", split_axis=0, concat_axis=0, tiled=True),
        lax.all_to_all(sent_grads, "dp", split_axis=0, concat_axis=0, tiled=True),
        lax.all_to_all(
            request.reshape(owners, capacity), "dp", split_axis=0, concat_axis=0, tiled=True
        ),
    )
    arrived_rows = arrived_rows.reshape(slots_all, block_rows, feat_width)
    arrived_grads = arrived_grads.reshape(slots_all, block_rows, head_width)
    arrived_tags = arrived_tags.reshape(slots_all)
    slot_local = jnp.maximum(arrived_tags - 1, 0)
    slot_down = down_weights[slot_local]
    slot_up = up_weights[slot_local]
    slot_scale = own_scale[slot_local]
    low_part = jnp.einsum(
        "stf,sfr->str", arrived_rows, slot_down, preferred_element_type=jnp.float32
    )
    back_part = jnp.einsum(
        "stk,srk->str", arrived_grads, slot_up, preferred_element_type=jnp.float32
    )
    low_full, back_full = (
        lax.psum(low_part.astype(jnp.bfloat16), "tensor").astype(jnp.float32),
        lax.psum(back_part.astype(jnp.bfloat16), "tensor").astype(jnp.float32),
    )
    reduced_scaled_rows = (slot_scale[:, None, None] * low_full).astype(jnp.bfloat16)
    backward_scaled_rows = (slot_scale[:, None, None] * back_full).astype(jnp.bfloat16)
    slot_values = jnp.einsum(
        "str,srk->stk", reduced_scaled_rows, slot_up, preferred_element_type=jnp.float32
    ).astype(jnp.bfloat16)
    slot_grads = jnp.einsum(
        "str,sfr->stf", backward_scaled_rows, slot_down, preferred_element_type=jnp.float32
    ).astype(jnp.bfloat16)
    down_pieces = jnp.einsum(
        "stf,str->sfr", arrived_rows, backward_scaled_rows, preferred_element_type=jnp.float32
    )
    up_pieces = jnp.einsum(
        "str,stk->srk", reduced_scaled_rows, arrived_grads, preferred_element_type=jnp.float32
    )
    down_matrix_gradient = tally_slots(arrived_tags, down_pieces, per_owner)
    up_matrix_gradient = tally_slots(arrived_tags, up_pieces, per_owner)
    returned_values, returned_grads = (
        lax.all_to_all(
            slot_values.reshape(owners, capacity, block_rows, head_width),
            "dp",
            split_axis=0,
            concat_axis=0,
            tiled=True,
        ),
        lax.all_to_all(
            slot_grads.reshape(owners, capacity, block_rows, feat_width),
            "dp",
            split_axis=0,
            concat_axis=0,
            tiled=True,
        ),
    )
    block_values = returned_values.reshape(slots_all, block_rows, head_width)[target]
    block_grads = returned_grads.reshape(slots_all, block_rows, feat_width)[target]
    base_part = jnp.dot(tokens, base_weight, preferred_element_type=jnp.float32)
    frozen_value_rows = lax.psum_scatter(
        base_part.astype(jnp.bfloat16), "tensor", scatter_dimension=1, tiled=True
    ).astype(jnp.float32)
    frozen_gradient_rows = lax.dot_general(
        lax.all_gather(cotangent, "tensor", axis=1, tiled=True),
        base_weight,
        (((1,), (1,)), ((), ())),
        preferred_element_type=jnp.float32,
    )
    values = (
        frozen_value_rows + block_values.reshape(tok_rows, head_width).astype(jnp.float32)
    ).astype(jnp.bfloat16)
    token_input_gradient = (
        frozen_gradient_rows + block_grads.reshape(tok_rows, feat_width).astype(jnp.float32)
    ).astype(jnp.bfloat16)
    return (values, token_input_gradient, down_matrix_gradient, up_matrix_gradient)


def solution(mesh):
    return jax.shard_map(
        on_device,
        mesh=mesh,
        in_specs=(
            P("dp", "tensor"),
            P("dp", "tensor"),
            P("tensor", None),
            P("dp", "tensor", None),
            P("dp", None, "tensor"),
            P("dp"),
            P(),
            P(),
        ),
        out_specs=(
            P("dp", "tensor"),
            P("dp", "tensor"),
            P("dp", "tensor", None),
            P("dp", None, "tensor"),
        ),
        check_vma=False,
    )
```

profile of v0, /device:TPU:6, one launch (start us, length us, event | category | flops | bytes accessed | tf_op | source)
XLA Modules:
  0.0 337.4 jit_solution(14315688301900957175)
XLA Ops:
  10.5 7.6 %all-to-all-start = ((s32[32,1,1]{2,1,0:T(1,128)}), s32[32,1,1]{2,1,0:T(1,128)S(1)}, u32[]{:S(2)}, u32[]{:S(2)}) async-start(s32[32,1,1]{2,1,0:T(1,128)} %copy.18), calls=%async_computation | async-start | bytes 32768 | tf_op jit(solution)/shard_map/all_to_all | solution.py:69
  18.2 2.7 gather_fusion.5
  23.6 7.1 %all-to-all-start.3 = ((bf16[32,1,128,128]{3,2,1,0:T(8,128)(2,1)}), bf16[32,1,128,128]{3,2,1,0:T(8,128)(2,1)}, u32[]{:S(2)}, u32[]{:S(2)}) async-start(bf16[32,1,128,128]{3,2,1,0:T(8,128)(2,1)} %bitcast_select_fusion.1), calls=%async_computation.3 | async-start | bytes 2097152 | tf_op jit(solution)/shard_map/all_to_all | solution.py:68
  30.6 3.5 %gather_fusion.1 = bf16[32,128,640]{2,1,0:T(8,128)(2,1)} fusion(bf16[16,128,640]{2,1,0:T(8,128)(2,1)S(1)} %bitcast.77, s32[1024]{0:T(1024)S(1)} %pad_clamp_fusion.2), kind=kCustom, calls=%fused_computation.1 | custom fusion | bytes 10485888 | tf_op jit(solution)/shard_map/gather | solution.py:51
  34.2 5.4 %bitcast_select_fusion = bf16[32,1,128,640]{3,2,1,0:T(8,128)(2,1)} fusion(bf16[32,128,640]{2,1,0:T(8,128)(2,1)} %gather_fusion.1, pred[32]{0:T(512)(128)(4,1)S(1)} %fusion.13), kind=kLoop, calls=%fused_computation.13 | loop fusion | flops 2621440 | bytes 10485792 | tf_op jit(solution)/shard_map/jit(_where)/select_n | solution.py:51
  39.5 6.4 %all-to-all-done.3 = bf16[32,1,128,128]{3,2,1,0:T(8,128)(2,1)} async-done(((bf16[32,1,128,128]{3,2,1,0:T(8,128)(2,1)}), bf16[32,1,128,128]{3,2,1,0:T(8,128)(2,1)}, u32[]{:S(2)}, u32[]{:S(2)}) %all-to-all-start.3) | async-done | bytes 1048608 | tf_op jit(solution)/shard_map/all_to_all | solution.py:68
  46.0 6.3 %all-to-all-start.1 = ((bf16[32,1,128,640]{3,2,1,0:T(8,128)(2,1)}), bf16[32,1,128,640]{3,2,1,0:T(8,128)(2,1)}, u32[]{:S(2)}, u32[]{:S(2)}) async-start(bf16[32,1,128,640]{3,2,1,0:T(8,128)(2,1)} %bitcast_select_fusion), calls=%async_computation.1 | async-start | bytes 10485760 | tf_op jit(solution)/shard_map/all_to_all | solution.py:67
  59.3 2.8 convolution_convert_fusion.2
  62.1 54.2 %all-to-all-done.1 = bf16[32,1,128,640]{3,2,1,0:T(8,128)(2,1)} async-done(((bf16[32,1,128,640]{3,2,1,0:T(8,128)(2,1)}), bf16[32,1,128,640]{3,2,1,0:T(8,128)(2,1)}, u32[]{:S(2)}, u32[]{:S(2)}) %all-to-all-start.1) | async-done | bytes 5242912 | tf_op jit(solution)/shard_map/all_to_all | solution.py:67
  116.3 6.2 %fusion.6 = bf16[32,128,64]{1,2,0:T(8,128)(2,1)} fusion(bf16[32,640,64]{1,2,0:T(8,128)(2,1)} %gather_fusion.2, bf16[32,1,128,640]{3,2,1,0:T(8,128)(2,1)} %all-to-all-done.1), kind=kOutput, calls=%fused_computation.22 | convolution fusion | flops 335806464 | bytes 8388608 | tf_op jit(solution)/shard_map/stf,sfr->str/dot_general | solution.py:80
  122.6 6.3 %convolution_convert_fusion = bf16[2048,1024]{1,0:T(8,128)(2,1)} fusion(bf16[2048,640]{1,0:T(8,128)(2,1)S(1)} %copy-done, bf16[640,1024]{1,0:T(8,128)(2,1)} %param.10), kind=kOutput, calls=%fused_computation.19 | convolution fusion | flops 2686451712 | bytes 8126464 | tf_op jit(solution)/shard_map/dot_general | solution.py:124
  128.9 6.5 %copy.21 = bf16[2048,1024]{0,1:T(8,128)(2,1)} copy(bf16[2048,1024]{1,0:T(8,128)(2,1)} %convolution_convert_fusion) | data formatting | bytes 8388608
  139.3 64.3 %all-reduce.3.cloned.1.call-done = (bf16[32,128,64]{1,2,0:T(8,128)(2,1)}, bf16[32,128,64]{1,2,0:T(8,128)(2,1)}) async-done(((bf16[32,128,64]{1,2,0:T(8,128)(2,1)}, bf16[32,128,64]{1,2,0:T(8,128)(2,1)}), (bf16[32,128,64]{1,2,0:T(8,128)(2,1)}, bf16[32,128,64]{1,2,0:T(8,128)(2,1)})) %all-reduce.3.cloned.1.call-update) | async-done | bytes 1048592 | tf_op jit(solution)/shard_map/psum | solution.py:87
  203.6 2.9 fusion.5
  206.4 7.5 %all-to-all-start.2 = ((bf16[32,1,128,128]{3,2,1,0:T(8,128)(2,1)}), bf16[32,1,128,128]{3,2,1,0:T(8,128)(2,1)}, u32[]{:S(2)}, u32[]{:S(2)}) async-start(bf16[32,1,128,128]{3,2,1,0:T(8,128)(2,1)} %fusion.5), calls=%async_computation.2 | async-start | bytes 2097152 | tf_op jit(solution)/shard_map/all_to_all | solution.py:107
  213.9 6.7 %convert_bitcast_fusion = bf16[32,1,128,640]{3,2,1,0:T(8,128)(2,1)} fusion(bf16[32,640,64]{1,2,0:T(8,128)(2,1)} %gather_fusion.2, bf16[32,128,64]{1,2,0:T(8,128)(2,1)} %get-tuple-element.19, f32[32]{0:T(128)S(1)} %compare_select_fusion.2), kind=kOutput, calls=%fused_computation.18 | convolution fusion | flops 338952192 | bytes 8388736 | tf_op jit(solution)/shard_map/str,sfr->stf/dot_general | solution.py:95
  220.7 8.6 %all-to-all-done.2 = bf16[32,1,128,128]{3,2,1,0:T(8,128)(2,1)} async-done(((bf16[32,1,128,128]{3,2,1,0:T(8,128)(2,1)}), bf16[32,1,128,128]{3,2,1,0:T(8,128)(2,1)}, u32[]{:S(2)}, u32[]{:S(2)}) %all-to-all-start.2) | async-done | bytes 1048608 | tf_op jit(solution)/shard_map/all_to_all | solution.py:107
  229.3 6.4 %all-to-all-start.4 = ((bf16[32,1,128,640]{3,2,1,0:T(8,128)(2,1)}), bf16[32,1,128,640]{3,2,1,0:T(8,128)(2,1)}, u32[]{:S(2)}, u32[]{:S(2)}) async-start(bf16[32,1,128,640]{3,2,1,0:T(8,128)(2,1)} %convert_bitcast_fusion), calls=%async_computation.4 | async-start | bytes 10485760 | tf_op jit(solution)/shard_map/all_to_all | solution.py:114
  240.5 4.9 %select_reduce_fusion.3 = (f32[640,64]{0,1:T(8,128)S(1)}, f32[640,64]{0,1:T(8,128)S(1)}, f32[640,64]{0,1:T(8,128)S(1)}, f32[640,64]{0,1:T(8,128)S(1)}) fusion(pred[32]{0:T(512)(128)(4,1)S(1)} %get-tuple-element.14, pred[32]{0:T(512)(128)(4,1)S(1)} %get-tuple-element.15, pred[32]{0:T(512)(128)(4,1)S(1)} %get-tuple-element.16, ...), kind=kOutput, calls=%fused_computation.17 | convolution fusion | flops 346652672 | bytes 6422784 | tf_op jit(solution)/shard_map/stf,str->sfr/dot_general | solution.py:98
  248.9 11.0 %reduce-scatter.4.cloned.1.call-done = bf16[128,2048]{1,0:T(8,128)(2,1)} async-done(((bf16[1024,2048]{1,0:T(8,128)(2,1)}), bf16[128,2048]{1,0:T(8,128)(2,1)}) %reduce-scatter.4.cloned.1.call-update) | async-done | bytes 524304
  263.2 36.4 %all-to-all-done.4 = bf16[32,1,128,640]{3,2,1,0:T(8,128)(2,1)} async-done(((bf16[32,1,128,640]{3,2,1,0:T(8,128)(2,1)}), bf16[32,1,128,640]{3,2,1,0:T(8,128)(2,1)}, u32[]{:S(2)}, u32[]{:S(2)}) %all-to-all-start.4) | async-done | bytes 5242912 | tf_op jit(solution)/shard_map/all_to_all | solution.py:114
  299.6 4.8 %gather_fusion.6 = bf16[16,128,640]{2,1,0:T(8,128)(2,1)} fusion(bf16[32,128,640]{2,1,0:T(8,128)(2,1)} %bitcast.20, s32[1024]{0:T(1024)S(1)} %pad_clamp_fusion), kind=kCustom, calls=%fused_computation.6 | custom fusion | bytes 5242944 | tf_op jit(solution)/shard_map/gather | solution.py:123
  304.4 18.1 %all-gather.2.cloned.1.call-done = bf16[2048,1024]{1,0:T(8,128)(2,1)} async-done(((bf16[2048,128]{1,0:T(8,128)(2,1)}), bf16[2048,1024]{1,0:T(8,128)(2,1)}) %all-gather.2.cloned.1.call-update) | async-done | bytes 4194320 | tf_op jit(solution)/shard_map/all_gather | solution.py:129
  322.5 8.4 %fusion = bf16[2048,640]{1,0:T(8,128)(2,1)} fusion(bf16[2048,640]{1,0:T(8,128)(2,1)} %bitcast.80, bf16[2048,1024]{1,0:T(8,128)(2,1)} %all-gather.2.cloned.1.call-done, bf16[640,1024]{1,0:T(8,128)(2,1)} %param.10), kind=kOutput, calls=%fused_computation.8 | convolution fusion | flops 2688286720 | bytes 10747904 | tf_op jit(solution)/shard_map/dot_general | solution.py:128
  (74 shorter events, 28.4 us)
Async XLA Ops:
  7.2 23.5 %copy-start = (bf16[2048,640]{1,0:T(8,128)(2,1)S(1)}, bf16[2048,640]{1,0:T(8,128)(2,1)}, u32[]{:S(2)}) copy-start(bf16[2048,640]{1,0:T(8,128)(2,1)} %param.8) | copy-start | bytes 7864324
  8.2 0.9 copy-start.13
  8.4 0.7 copy-start.15
  10.5 13.0 %all-to-all-start = ((s32[32,1,1]{2,1,0:T(1,128)}), s32[32,1,1]{2,1,0:T(1,128)S(1)}, u32[]{:S(2)}, u32[]{:S(2)}) async-start(s32[32,1,1]{2,1,0:T(1,128)} %copy.18), calls=%async_computation | async-start | bytes 32768 | tf_op jit(solution)/shard_map/all_to_all | solution.py:69
  23.6 22.4 %all-to-all-start.3 = ((bf16[32,1,128,128]{3,2,1,0:T(8,128)(2,1)}), bf16[32,1,128,128]{3,2,1,0:T(8,128)(2,1)}, u32[]{:S(2)}, u32[]{:S(2)}) async-start(bf16[32,1,128,128]{3,2,1,0:T(8,128)(2,1)} %bitcast_select_fusion.1), calls=%async_computation.3 | async-start | bytes 2097152 | tf_op jit(solution)/shard_map/all_to_all | solution.py:68
  39.5 12.8 %copy-start.11 = (s32[128]{0:T(128)S(1)}, s32[128]{0:T(128)}, u32[]{:S(2)}) copy-start(s32[128]{0:T(128)} %param.15) | copy-start | bytes 1540
  39.5 12.8 %copy-start.12 = (s32[128]{0:T(128)S(1)}, s32[128]{0:T(128)}, u32[]{:S(2)}) copy-start(s32[128]{0:T(128)} %param.14) | copy-start | bytes 1540
  39.5 13.5 %copy-start.3 = (f32[4,64,128]{2,1,0:T(8,128)S(1)}, f32[4,64,128]{2,1,0:T(8,128)}, u32[]{:S(2)}) copy-start(f32[4,64,128]{2,1,0:T(8,128)} %param.12) | copy-start | bytes 393220
  46.0 70.3 %all-to-all-start.1 = ((bf16[32,1,128,640]{3,2,1,0:T(8,128)(2,1)}), bf16[32,1,128,640]{3,2,1,0:T(8,128)(2,1)}, u32[]{:S(2)}, u32[]{:S(2)}) async-start(bf16[32,1,128,640]{3,2,1,0:T(8,128)(2,1)} %bitcast_select_fusion), calls=%async_computation.1 | async-start | bytes 10485760 | tf_op jit(solution)/shard_map/all_to_all | solution.py:67
  52.3 151.3 %all-reduce.3.cloned.1.call-start = ((), (), s32[]{:S(2)}) async-start(), calls=%async_computation.8 | async-start | bytes 2097152 | tf_op jit(solution)/shard_map/psum | solution.py:87
  55.0 0.5 copy-start.7
  55.6 0.6 copy-start.4
  122.6 137.3 %reduce-scatter.4.cloned.1.call-start = ((), (), s32[]{:S(2)}) async-start(), calls=%async_computation.7 | async-start | bytes 4718592
  135.4 0.8 copy-start.10
  135.4 1.4 copy-start.8
  135.4 187.0 %all-gather.2.cloned.1.call-start = ((), (), s32[]{:S(2)}) async-start(), calls=%async_computation.6 | async-start | bytes 4718592 | tf_op jit(solution)/shard_map/all_gather | solution.py:129
  139.2 74.7 %copy-start.5 = (f32[32]{0:T(128)}, f32[32]{0:T(128)S(1)}, u32[]{:S(2)}) copy-start(f32[32]{0:T(128)S(1)} %compare_select_fusion.2) | copy-start | bytes 388
  206.4 22.8 %all-to-all-start.2 = ((bf16[32,1,128,128]{3,2,1,0:T(8,128)(2,1)}), bf16[32,1,128,128]{3,2,1,0:T(8,128)(2,1)}, u32[]{:S(2)}, u32[]{:S(2)}) async-start(bf16[32,1,128,128]{3,2,1,0:T(8,128)(2,1)} %fusion.5), calls=%async_computation.2 | async-start | bytes 2097152 | tf_op jit(solution)/shard_map/all_to_all | solution.py:107
  220.7 14.9 %copy-start.14 = (s32[16]{0:T(128)S(1)}, s32[16]{0:T(128)}, u32[]{:S(2)}) copy-start(s32[16]{0:T(128)} %copy-done.13) | copy-start | bytes 196
  220.7 15.0 %copy-start.16 = (s32[16]{0:T(128)S(1)}, s32[16]{0:T(128)}, u32[]{:S(2)}) copy-start(s32[16]{0:T(128)} %copy-done.15) | copy-start | bytes 196
  220.7 17.4 %copy-start.2 = (bf16[32,128,64]{1,2,0:T(8,128)(2,1)S(1)}, bf16[32,128,64]{1,2,0:T(8,128)(2,1)}, u32[]{:S(2)}) copy-start(bf16[32,128,64]{1,2,0:T(8,128)(2,1)} %get-tuple-element.18) | copy-start | bytes 1572868
  220.7 17.4 %copy-start.6 = (f32[32]{0:T(128)S(1)}, f32[32]{0:T(128)}, u32[]{:S(2)}) copy-start(f32[32]{0:T(128)} %copy-done.5) | copy-start | bytes 388
  229.3 70.3 %all-to-all-start.4 = ((bf16[32,1,128,640]{3,2,1,0:T(8,128)(2,1)}), bf16[32,1,128,640]{3,2,1,0:T(8,128)(2,1)}, u32[]{:S(2)}, u32[]{:S(2)}) async-start(bf16[32,1,128,640]{3,2,1,0:T(8,128)(2,1)} %convert_bitcast_fusion), calls=%async_computation.4 | async-start | bytes 10485760 | tf_op jit(solution)/shard_map/all_to_all | solution.py:114
  235.6 4.9 %copy-start.1 = (bf16[32,128,64]{1,2,0:T(8,128)(2,1)S(1)}, bf16[32,128,64]{1,2,0:T(8,128)(2,1)}, u32[]{:S(2)}) copy-start(bf16[32,128,64]{1,2,0:T(8,128)(2,1)} %get-tuple-element.19) | copy-start | bytes 1572868
  (1 other events, 0.5 us)
Sparse Core Ops, SparseCore 0:
  122.7 80.8 all-reduce.2
  206.1 53.6 reduce-scatter.3
  261.6 60.8 all-gather.1
where the time goes:
time: 339 us; the launch traced here: 337 us
  waiting for transfers between devices  200 us (59%)
  matrix products  40 us (12%)
  starting transfers between devices  35 us (10%)
  local copies, waits for them, and re-layouts  28.2 us (8%)
  other arithmetic  20.1 us (6%)
  between operations  14 us (4%)
    psum x1, waiting for transfers between devices, on_device(): lax.psum(low_part.astype(jnp.bfloat16), 'tensor').astype(jnp.float32)  64.3 us
    all_to_all x1, waiting for transfers between devices, on_device(): lax.all_to_all(sent_rows, 'dp', split_axis=0, concat_axis=0, tiled=True)  54.2 us
    all_to_all x1, waiting for transfers between devices, on_device(): lax.all_to_all(slot_grads.reshape(owners, capacity, block_rows, feat_widt...  36.4 us
    all_gather x1, waiting for transfers between devices, on_device(): lax.all_gather(cotangent, 'tensor', axis=1, tiled=True)  18.1 us
    unnamed x4, waiting for transfers between devices  11.7 us
    unnamed x36, local copies, waits for them, and re-layouts  9.39 us
    all_to_all x1, waiting for transfers between devices, on_device(): lax.all_to_all(slot_values.reshape(owners, capacity, block_rows, head_wid...  8.56 us
    dot_general x1, matrix products, on_device(): lax.dot_general(lax.all_gather(cotangent, 'tensor', axis=1, tiled=True),...  8.35 us
  transfers between devices with their start and end apart: 8, of which 8 were waited for; matrix products, arithmetic and copies ran while one was open for 20% of the time, Pallas kernels for 0%

commit v1 on v0

v1 whole, which is shorter than its diff:
```python
import functools

import jax
import jax.numpy as jnp
from jax import lax
from jax.experimental import pallas as pl
from jax.experimental.pallas import tpu as pltpu
from jax.sharding import PartitionSpec as P

MESH = pl.DeviceIdType.MESH
BF, F32, I32 = jnp.bfloat16, jnp.float32, jnp.int32
DP, NZ = 32, 8
ROWS, FEAT, HEAD, R, BLK, NB, OWN = 2048, 640, 128, 64, 128, 16, 4
CH = 256
NC = ROWS // CH
MSG = 3 * NC + NC // 2
DEPTH = 4
LAST = MSG // 2
T_UP = 4
T_BACK = T_UP + 1
T_DOWN = 16
T_LOW = T_DOWN + 1


def dot(a, b, ca, cb):
    return lax.dot_general(a, b, (((ca,), (cb,)), ((), ())), preferred_element_type=F32)


def kernel(
    ba_s, slot_s, rank_s, slot_v, rank_v, tok_h, cot_h, w_h, dn_h, up_h,
    val_o, tig_o, dmg_o, umg_o,
    tok, cotf, w, dnf, upf, dnb, upb, base, rsr, reqs, tagr, tag_v, bi_v, scale,
    usend, urecv, dsend, drecv, gsend, grecv, hsend, hrecv, grads, hgrads,
    arp, arr, tot, scaled, lorav, valv, tigv, dacc, uacc, tag_s, bi_s,
    in_sem, out_sem, ag_s, ag_r, rs_s, rs_r, ar_s, ar_r, tg_s, tg_r,
    us_s, us_r, ds_s, ds_r, gs_s, gs_r, hs_s, hs_r, sm_sem,
):
    d = lax.axis_index("dp")
    z = lax.axis_index("tensor")
    x, y, c = d // 8, (d // 2) % 4, d % 2
    right, left = (z + 1) % NZ, (z + NZ - 1) % NZ

    cp_cot = pltpu.make_async_copy(cot_h, cotf.at[z], in_sem.at[0])
    cp_up = pltpu.make_async_copy(up_h, upf, in_sem.at[1])
    cp_dn = pltpu.make_async_copy(dn_h, dnf, in_sem.at[2])
    cp_tok = pltpu.make_async_copy(tok_h, tok, in_sem.at[3])
    cp_w = pltpu.make_async_copy(w_h, w, in_sem.at[4])
    for cp in (cp_cot, cp_up, cp_dn, cp_tok, cp_w):
        cp.start()

    barrier = pltpu.get_barrier_semaphore()

    def greet(i, carry):
        pl.semaphore_signal(barrier, inc=1, device_id=((d + i) % DP, z), device_id_type=MESH)
        return carry

    lax.fori_loop(1, DP, greet, 0)
    for to in (right, left):
        pl.semaphore_signal(barrier, inc=1, device_id=(d, to), device_id_type=MESH)

    own3 = lax.broadcasted_iota(I32, (DP, 8, 128), 0)
    own2 = lax.broadcasted_iota(I32, (DP, 128), 0)
    pair2 = lax.broadcasted_iota(I32, (8, 128), 0)
    lane2 = lax.broadcasted_iota(I32, (8, 128), 1)
    tags = jnp.zeros((DP, 8, 128), I32)
    which = jnp.zeros((DP, 128), I32)
    ranks = jnp.ones((8, 128), I32)
    for b in range(NB):
        a = ba_s[b]
        s = slot_s[a]
        o = s // OWN
        tags = jnp.where(own3 == o, s - o * OWN + 1, tags)
        which = jnp.where(own2 == o, b, which)
        here = (pair2 == b // 2) & ((lane2 >= R) if b % 2 else (lane2 < R))
        ranks = jnp.where(here, rank_s[a], ranks)
    reqs[...] = tags
    bi_v[...] = which
    scale[...] = R / (4.0 * ranks.astype(F32))
    cp_bi = pltpu.make_async_copy(bi_v, bi_s, sm_sem.at[0])
    cp_bi.start()
    pl.semaphore_wait(barrier, DP + 1)

    def ag(m, dirn):
        h, cc = m // NC, m % NC
        row = cc * CH
        if dirn == 0:
            shard, to = (z - h + NZ) % NZ, right
        else:
            shard, to = (z + h) % NZ, left
            row = row + (h // 3) * (ROWS // 2)
        part = cotf.at[shard, pl.ds(pl.multiple_of(row, CH), CH)]
        return pltpu.make_async_remote_copy(
            src_ref=part, dst_ref=part, send_sem=ag_s.at[dirn, m], recv_sem=ag_r.at[dirn, m],
            device_id=(d, to), device_id_type=MESH)

    cp_cot.wait()

    def ag_first(m, carry):
        ag(m, 0).start()
        ag(m, 1).start()
        return carry

    lax.fori_loop(0, DEPTH, ag_first, 0)

    def xmsg(i, src, dst, ss, rs):
        j = (i * 13) % DP
        px, py, pc = (x + j // 8) % 4, (y + (j // 2) % 4) % 4, (c + j % 2) % 2
        t = px * 8 + py * 2 + pc
        return t, pltpu.make_async_remote_copy(
            src_ref=src.at[t], dst_ref=dst.at[d], send_sem=ss.at[i], recv_sem=rs.at[i],
            device_id=(t, z), device_id_type=MESH)

    def x_recv(src, dst, ss, rs):
        def go(i, carry):
            xmsg(i, src, dst, ss, rs)[1].wait_recv()
            return carry
        lax.fori_loop(1, DP, go, 0)

    def x_sent(src, dst, ss, rs):
        def go(i, carry):
            xmsg(i, src, dst, ss, rs)[1].wait_send()
            return carry
        lax.fori_loop(1, DP, go, 0)

    tg = (reqs, tagr, tg_s, tg_r)
    us = (usend, urecv, us_s, us_r)
    ds = (dsend, drecv, ds_s, ds_r)
    gs = (gsend, grecv, gs_s, gs_r)
    hs = (hsend, hrecv, hs_s, hs_r)

    def tag_go(i, carry):
        xmsg(i, *tg)[1].start()
        return carry

    lax.fori_loop(1, DP, tag_go, 0)
    tagr[d] = reqs[d]

    cp_up.wait()
    cp_dn.wait()
    for l in range(OWN):
        mine = slot_v[...] == d * OWN + l
        rank = jnp.sum(jnp.where(mine, rank_v[...], 0), axis=1, keepdims=True)
        upb[l] = jnp.where(lax.broadcasted_iota(I32, (R, HEAD), 0) < rank, upf[l], 0.0).astype(BF)
        dnb[l] = jnp.where(lax.broadcasted_iota(I32, (R, FEAT), 0) < rank, dnf[l], 0.0).astype(BF)
    x_recv(*tg)
    tag_v[...] = tagr[:, 0, :]
    cp_tag = pltpu.make_async_copy(tag_v, tag_s, sm_sem.at[1])
    cp_tag.start()
    cp_tag.wait()

    def fill(src, args):
        def go(i, carry):
            t, copy = xmsg(i, *args)
            args[0][t] = src[jnp.maximum(tag_s[t, 0] - 1, 0)]
            copy.start()
            return carry
        lax.fori_loop(1, DP, go, 0)
        args[1][d] = src[jnp.maximum(tag_s[d, 0] - 1, 0)]

    fill(upb, us)
    fill(dnb, ds)
    cp_bi.wait()
    cp_tok.wait()
    cp_w.wait()

    def owner_of(b):
        return slot_s[ba_s[b]] // OWN

    half = (slice(0, BLK // 2), slice(BLK // 2, BLK))

    def ar_copy(q, k, dirn, src, dst):
        return pltpu.make_async_remote_copy(
            src_ref=src, dst_ref=dst, send_sem=ar_s.at[q, dirn, k], recv_sem=ar_r.at[q, dirn, k],
            device_id=(d, (right, left)[dirn]), device_id_type=MESH)

    def ar_msg(q, k, dirn):
        sgn = (1, -1)[dirn]
        if k == 0:
            p = (z + 4) % NZ
            lo = (0, BLK // 2)[dirn]
            return ar_copy(q, k, dirn, arp.at[q, p, pl.ds(lo, BLK // 2)], arr.at[q, dirn, 0, pl.ds(lo, BLK // 2)])
        if k < 4:
            p = (z + sgn * (4 - k) + NZ) % NZ
            return ar_copy(q, k, dirn, arp.at[q, p], arr.at[q, dirn, k])
        p = (z - sgn * (k - 4) + NZ) % NZ
        if k < 7:
            return ar_copy(q, k, dirn, tot.at[q, p], tot.at[q, p])
        lo = (0, BLK // 2)[dirn]
        part = tot.at[q, p, pl.ds(lo, BLK // 2)]
        return ar_copy(q, k, dirn, part, part)

    def ar_step(q, k):
        if k > 0:
            for dirn in (0, 1):
                ar_msg(q, k - 1, dirn).wait_recv()
        if k in (1, 2, 3):
            for dirn in (0, 1):
                p = (z + (1, -1)[dirn] * (4 - k) + NZ) % NZ
                rows = half[dirn] if k == 1 else slice(0, BLK)
                arp[q, p, rows] = (arp[q, p, rows].astype(F32) + arr[q, dirn, k - 1, rows].astype(F32)).astype(BF)
        if k == 4:
            tot[q, z] = (arp[q, z].astype(F32) + arr[q, 0, 3].astype(F32) + arr[q, 1, 3].astype(F32)).astype(BF)
        if k < 8:
            for dirn in (0, 1):
                ar_msg(q, k, dirn).start()

    def scale_all(q):
        def go(j, carry):
            scaled[q, j] = (scale[pl.ds(j, 1), :] * tot[q, j].astype(F32)).astype(BF)
            return carry
        lax.fori_loop(0, NZ, go, 0)

    lanes = lax.broadcasted_iota(I32, (BLK, 2 * R), 1)

    def rows_of(b, n=BLK):
        return pl.ds(pl.multiple_of(b * n, n), n)

    def back_partial():
        x_recv(*us)

        def go(j, carry):
            parts = []
            for k in (0, 1):
                b = 2 * j + k
                parts.append(dot(cotf[z, rows_of(b), :], urecv[owner_of(b)], 1, 1))
            arp[0, j] = jnp.concatenate(parts, axis=1).astype(BF)
            return carry

        lax.fori_loop(0, NZ, go, 0)

    def low_partial():
        x_recv(*ds)

        def go(j, carry):
            parts = []
            for k in (0, 1):
                b = 2 * j + k
                parts.append(dot(tok[rows_of(b), :], drecv[owner_of(b)], 1, 1))
            arp[1, j] = jnp.concatenate(parts, axis=1).astype(BF)
            return carry

        lax.fori_loop(0, NZ, go, 0)

    def send_grads(src, args):
        def go(i, carry):
            t, copy = xmsg(i, *args)
            args[0][t] = src[bi_s[t, 0]]
            copy.start()
            return carry
        lax.fori_loop(1, DP, go, 0)
        args[1][d] = src[bi_s[d, 0]]

    def down_grads():
        scale_all(0)

        def go(j, carry):
            turned = jnp.transpose(scaled[0, j].astype(F32)).astype(BF)
            for k in (0, 1):
                b = 2 * j + k
                grads[b] = dot(turned[k * R:(k + 1) * R], tok[rows_of(b), :], 1, 0).astype(BF)
            return carry

        lax.fori_loop(0, NZ, go, 0)
        send_grads(grads, gs)

    def up_grads():
        scale_all(1)

        def go(j, carry):
            mine = scaled[1, j]
            turned = jnp.transpose(mine.astype(F32)).astype(BF)
            ups = jnp.concatenate([urecv[owner_of(2 * j)], urecv[owner_of(2 * j + 1)]], axis=0)
            for k in (0, 1):
                b = 2 * j + k
                hgrads[b] = dot(turned[k * R:(k + 1) * R], cotf[z, rows_of(b), :], 1, 0).astype(BF)
                only = jnp.where((lanes >= R) if k else (lanes < R), mine, jnp.zeros((), BF))
                lorav[rows_of(b), :] = dot(only, ups, 1, 0).astype(BF)
            return carry

        lax.fori_loop(0, NZ, go, 0)
        send_grads(hgrads, hs)

    def base_chunk(cc):
        rows = rows_of(cc, CH)
        part = dot(tok[rows, :], w[...], 1, 0)
        for k in range(NZ):
            base[k, rows, :] = part[:, k * HEAD:(k + 1) * HEAD].astype(BF)

    def tig_out(cc):
        rows = rows_of(cc, CH)
        return pltpu.make_async_copy(tigv.at[rows], tig_o.at[rows], out_sem.at[cc])

    def tig_chunk(cc):
        rows = rows_of(cc, CH)
        full = jnp.concatenate([cotf[k, rows, :] for k in range(NZ)], axis=1)
        part = dot(full, w[...], 1, 1)
        mine = scaled[0, cc]
        dns = jnp.concatenate([drecv[owner_of(2 * cc)], drecv[owner_of(2 * cc + 1)]], axis=0)
        zero = jnp.zeros((), BF)
        both = jnp.concatenate([jnp.where(lanes < R, mine, zero), jnp.where(lanes >= R, mine, zero)], axis=0)
        lora = dot(both, dns, 1, 0).astype(BF).astype(F32)
        tigv[rows, :] = (part + lora).astype(BF)
        tig_out(cc).start()

    def rs(n, h, cc, dirn):
        rows = rows_of(cc, CH)
        if dirn == 0:
            dest, to = (z + h) % NZ, right
        else:
            dest, to = (z - h + NZ) % NZ, left
        return pltpu.make_async_remote_copy(
            src_ref=base.at[dest, rows], dst_ref=rsr.at[dirn, n], send_sem=rs_s.at[dirn, n],
            recv_sem=rs_r.at[dirn, n], device_id=(d, to), device_id_type=MESH)

    def rs_add(n_in, h, cc, dirn):
        rs(n_in, h, cc, dirn).wait_recv()
        dest = (z + h) % NZ if dirn == 0 else (z - h + NZ) % NZ
        rows = rows_of(cc, CH)
        base[dest, rows, :] = (base[dest, rows, :].astype(F32) + rsr[dirn, n_in].astype(F32)).astype(BF)

    def ag_step(m):
        for dirn in (0, 1):
            lag = NC - (m // (3 * NC)) * (NC // 2) * dirn

            @pl.when(m >= NC)
            def _():
                ag(m - lag, dirn).wait_recv()
            ag(m - DEPTH, dirn).wait_send()
            ag(m, dirn).start()

    def rs_step(n):
        @pl.when(n < 4)
        def _():
            for dirn in (0, 1):
                ag(MSG - DEPTH + n, dirn).wait_send()
                rs(n, 4, n + dirn * 4, dirn).start()

        @pl.when(n >= 4)
        def _():
            k, cc = (n - 4) // NC, (n - 4) % NC
            for dirn in (0, 1):
                @pl.when((k == 0) & (cc // 4 == dirn))
                def _():
                    rs_add(cc - 4 * dirn, 3, cc, dirn)

                @pl.when(k > 0)
                def _():
                    rs_add(n - NC, 3 - k, cc, dirn)
                rs(n - DEPTH, 3, cc, dirn).wait_send()
                rs(n, 3 - k, cc, dirn).start()

    def tick_a(t, carry):
        ag_step(2 * t)
        ag_step(2 * t + 1)

        @pl.when(t == T_UP)
        def _():
            back_partial()

        for k in range(8):
            @pl.when(t == T_BACK + k)
            def _():
                ar_step(0, k)

        @pl.when(t >= LAST - NC)
        def _():
            base_chunk(t - (LAST - NC))
        return carry

    lax.fori_loop(DEPTH // 2, LAST, tick_a, 0)
    ar_step(0, 8)
    down_grads()

    def ag_rest(m, carry):
        ag(m, 0).wait_recv()
        ag(m - NC // 2 + (m // (3 * NC)) * (NC // 2), 1).wait_recv()
        return carry

    def tick_b(t, carry):
        rs_step(2 * (t - LAST))
        rs_step(2 * (t - LAST) + 1)

        @pl.when(t == LAST + 1)
        def _():
            lax.fori_loop(MSG - NC, MSG, ag_rest, 0)

        @pl.when(t == T_DOWN)
        def _():
            low_partial()

        for k in range(9):
            @pl.when(t == T_LOW + k)
            def _():
                ar_step(1, k)

        @pl.when((t > T_DOWN) & (t <= T_DOWN + NC))
        def _():
            tig_chunk(t - T_DOWN - 1)

        @pl.when(t == T_LOW + 8)
        def _():
            up_grads()
        return carry

    lax.fori_loop(LAST, 2 * LAST, tick_b, 0)

    def finish(cc, carry):
        n = MSG - NC + cc
        rows = rows_of(cc, CH)
        for dirn in (0, 1):
            rs(n, 1, cc, dirn).wait_recv()
        whole = base[z, rows, :].astype(F32) + rsr[0, n].astype(F32) + rsr[1, n].astype(F32)
        valv[rows, :] = (whole + lorav[rows, :].astype(F32)).astype(BF)
        return carry

    lax.fori_loop(0, NC, finish, 0)
    cp_val = pltpu.make_async_copy(valv, val_o, out_sem.at[NC])
    cp_val.start()

    def tally(recv, acc, rows, width):
        def tile(r, carry):
            here = pl.ds(pl.multiple_of(r * rows, rows), rows)

            def add(s, sums):
                tag = tag_s[s, 0]
                piece = recv[s, here, :].astype(F32)
                return tuple(
                    sums[l] + jnp.where(tag == l + 1, piece, 0.0) for l in range(OWN))

            zero = jnp.zeros((rows, width), F32)
            sums = lax.fori_loop(0, DP, add, (zero,) * OWN)
            for l in range(OWN):
                acc[l, here, :] = sums[l]
            return carry
        lax.fori_loop(0, R // rows, tile, 0)

    x_recv(*gs)
    tally(grecv, dacc, 16, FEAT)
    cp_dm = pltpu.make_async_copy(dacc, dmg_o, out_sem.at[NC + 1])
    cp_dm.start()
    x_recv(*hs)
    tally(hrecv, uacc, 64, HEAD)
    cp_um = pltpu.make_async_copy(uacc, umg_o, out_sem.at[NC + 2])
    cp_um.start()

    def rs_rest(n, carry):
        for dirn in (0, 1):
            rs(n, 3, 0, dirn).wait_send()
        return carry

    lax.fori_loop(MSG - DEPTH, MSG, rs_rest, 0)
    for args in (tg, us, ds, gs, hs):
        x_sent(*args)
    for q in (0, 1):
        for k in range(8):
            for dirn in (0, 1):
                ar_msg(q, k, dirn).wait_send()

    def tig_rest(cc, carry):
        tig_out(cc).wait()
        return carry

    lax.fori_loop(0, NC, tig_rest, 0)
    cp_val.wait()
    cp_dm.wait()
    cp_um.wait()


def on_device(tokens, cotangent, base_weight, adapter_down, adapter_up, block_adapter, adapter_slot, adapter_rank):
    vm, dma = pltpu.VMEM, pltpu.SemaphoreType.DMA
    smem = pl.BlockSpec(memory_space=pltpu.SMEM)
    vmem = pl.BlockSpec(memory_space=pltpu.VMEM)
    hbm = pl.BlockSpec(memory_space=pl.ANY)
    scratch = [
        vm((ROWS, FEAT), BF), vm((NZ, ROWS, HEAD), BF), vm((FEAT, NZ * HEAD), BF),
        vm((OWN, R, FEAT), F32), vm((OWN, R, HEAD), F32), vm((OWN, R, FEAT), BF), vm((OWN, R, HEAD), BF),
        vm((NZ, ROWS, HEAD), BF), vm((2, MSG, CH, HEAD), BF),
        vm((DP, 8, 128), I32), vm((DP, 8, 128), I32), vm((DP, 128), I32), vm((DP, 128), I32), vm((8, 128), F32),
        vm((DP, R, HEAD), BF), vm((DP, R, HEAD), BF),
        vm((DP, R, FEAT), BF), vm((DP, R, FEAT), BF),
        vm((DP, R, FEAT), BF), vm((DP, R, FEAT), BF),
        vm((DP, R, HEAD), BF), vm((DP, R, HEAD), BF),
        vm((NB, R, FEAT), BF), vm((NB, R, HEAD), BF),
        vm((2, NZ, BLK, 2 * R), BF), vm((2, 2, 4, BLK, 2 * R), BF), vm((2, NZ, BLK, 2 * R), BF), vm((2, NZ, BLK, 2 * R), BF),
        vm((ROWS, HEAD), BF), vm((ROWS, HEAD), BF), vm((ROWS, FEAT), BF),
        vm((OWN, R, FEAT), F32), vm((OWN, R, HEAD), F32),
        pltpu.SMEM((DP, 128), I32), pltpu.SMEM((DP, 128), I32),
        dma((5,)), dma((NC + 3,)),
        dma((2, MSG)), dma((2, MSG)), dma((2, MSG)), dma((2, MSG)),
        dma((2, 2, 8)), dma((2, 2, 8)),
        dma((DP,)), dma((DP,)), dma((DP,)), dma((DP,)), dma((DP,)), dma((DP,)),
        dma((DP,)), dma((DP,)), dma((DP,)), dma((DP,)), dma((2,)),
    ]
    val, tig, dmg, umg = pl.pallas_call(
        kernel,
        out_shape=(
            jax.ShapeDtypeStruct((ROWS, HEAD), BF),
            jax.ShapeDtypeStruct((ROWS, FEAT), BF),
            jax.ShapeDtypeStruct((OWN, R, FEAT), F32),
            jax.ShapeDtypeStruct((OWN, R, HEAD), F32),
        ),
        in_specs=[smem, smem, smem, vmem, vmem, hbm, hbm, hbm, hbm, hbm],
        out_specs=(hbm, hbm, hbm, hbm),
        scratch_shapes=scratch,
        compiler_params=pltpu.CompilerParams(
            collective_id=0, has_side_effects=True, vmem_limit_bytes=54 * 2**20),
    )(
        block_adapter, adapter_slot, adapter_rank,
        adapter_slot.reshape(1, -1), adapter_rank.reshape(1, -1),
        tokens, cotangent, base_weight, jnp.swapaxes(adapter_down, 1, 2), adapter_up,
    )
    return val, tig, jnp.swapaxes(dmg, 1, 2), umg


def solution(mesh):
    return jax.shard_map(
        on_device,
        mesh=mesh,
        in_specs=(
            P("dp", "tensor"), P("dp", "tensor"), P("tensor", None), P("dp", "tensor", None),
            P("dp", None, "tensor"), P("dp"), P(), P(),
        ),
        out_specs=(P("dp", "tensor"), P("dp", "tensor"), P("dp", "tensor", None), P("dp", None, "tensor")),
        check_vma=False,
    )
```

time: 339 us -> 140 us (0.41)
  waiting for transfers between devices: 200 us -> 0 us
  Pallas kernels: 0 us -> 132 us
  matrix products: 40 us -> 0 us
  starting transfers between devices: 35 us -> 0 us
  local copies, waits for them, and re-layouts: 28.2 us -> 6.9 us
  other arithmetic: 20.1 us -> 0 us
  between operations: 14 us -> 0.65 us
    pallas_call x0 -> x1, Pallas kernels: none -> 132 us  [on_device(): pl.pallas_call(kernel, out_shape=(jax.ShapeDtypeStruct((ROWS, HEAD), BF),...]
    all_to_all x5 -> x0, waiting for transfers between devices: 106 us -> none  [the longest x1 54.2 us: on_device(): lax.all_to_all(sent_rows, 'dp', split_axis=0, concat_axis=0, tiled=True)]
    psum x1 -> x0, waiting for transfers between devices: 64.3 us -> none  [on_device(): lax.psum(low_part.astype(jnp.bfloat16), 'tensor').astype(jnp.float32)]
    dot_general x8 -> x0, matrix products: 40 us -> none  [the longest x1 8.35 us: on_device(): lax.dot_general(lax.all_gather(cotangent, 'tensor', axis=1, tiled=True),...]
    all_to_all x5 -> x0, starting transfers between devices: 34.9 us -> none  [the longest x1 7.61 us: on_device(): lax.all_to_all(request.reshape(owners, capacity), 'dp', split_axis=0, con...]
    gather x8 -> x0, local copies, waits for them, and re-layouts: 18.1 us -> none  [the longest x2 6.23 us: gather_slots(): block_array[source_block]]
    all_gather x1 -> x0, waiting for transfers between devices: 18.1 us -> none  [on_device(): lax.all_gather(cotangent, 'tensor', axis=1, tiled=True)]
    unnamed x4 -> x0, waiting for transfers between devices: 11.7 us -> none
  transfers between devices with their start and end apart: 8 -> 0, of which waited for: 8 -> 0; matrix products, arithmetic and copies ran while one was open for 20% -> 0% of each run, Pallas kernels for 0% -> 0%
where the time goes in v1:
time: 140 us; the launch traced here: 139 us
  Pallas kernels  132 us (94%)
  local copies, waits for them, and re-layouts  6.9 us (5%)
    pallas_call x1, Pallas kernels, on_device(): pl.pallas_call(kernel, out_shape=(jax.ShapeDtypeStruct((ROWS, HEAD), BF),...  132 us
    unnamed x8, local copies, waits for them, and re-layouts  6.9 us

profile of v1, /device:TPU:6, one launch (start us, length us, event | category | flops | bytes accessed | tf_op | source)
XLA Modules:
  0.0 139.4 jit_solution(17143530045002915991)
XLA Ops:
  0.6 131.9 %shard_map.111 = (bf16[2048,128]{1,0:T(8,128)(2,1)}, bf16[2048,640]{1,0:T(8,128)(2,1)}, f32[4,64,640]{2,1,0:T(8,128)}, f32[4,64,128]{2,1,0:T(8,128)}) custom-call(s32[16]{0:T(128)} %ba_s.1, s32[128]{0:T(128)} %slot_s.1, s32[128]{0:T(128)} %rank_s.1, s32[1,128]{1,0:T(1,128)} %bitcast.6, s32[1,128]{1,0:T(1,128)} %bitcast.7, bf16[2048,640]{1,0:T(8,128)(2,1)} %tok_h.1, ...), custom_call_target="tpu_custom_call" | custom-call | tf_op jit(solution)/shard_map/pallas_call | solution.py:494
  132.5 1.9 %copy.16 = bf16[2048,128]{1,0:T(8,128)(2,1)} copy(bf16[2048,128]{1,0:T(8,128)(2,1)} %get-tuple-element.16) | data formatting | bytes 1048576
  134.4 0.0 copy-start
  134.4 0.0 copy-start.1
  134.4 3.5 %copy.17 = bf16[2048,640]{1,0:T(8,128)(2,1)} copy(bf16[2048,640]{1,0:T(8,128)(2,1)} %get-tuple-element.17) | data formatting | bytes 5242880
  137.9 0.0 copy-done
  137.9 0.8 copy.18
  138.8 0.0 copy-done.1
  138.8 0.7 copy.19
Async XLA Ops:
  134.4 3.5 %copy-start = (f32[4,64,640]{2,1,0:T(8,128)S(1)}, f32[4,64,640]{2,1,0:T(8,128)}, u32[]{:S(2)}) copy-start(f32[4,64,640]{2,1,0:T(8,128)} %get-tuple-element.10) | copy-start | bytes 1966084
  134.4 4.4 %copy-start.1 = (f32[4,64,128]{2,1,0:T(8,128)S(1)}, f32[4,64,128]{2,1,0:T(8,128)}, u32[]{:S(2)}) copy-start(f32[4,64,128]{2,1,0:T(8,128)} %get-tuple-element.19) | copy-start | bytes 393220

commit v2 on v1

--- a/solution.py
+++ b/solution.py
@@ -16,10 +16,12 @@
 MSG = 3 * NC + NC // 2
 DEPTH = 4
 LAST = MSG // 2
-T_UP = 4
+T_UP = 5
 T_BACK = T_UP + 1
-T_DOWN = 16
+T_HAND = 6
+T_DOWN = 15
 T_LOW = T_DOWN + 1
+T_TALLY = 22
 
 
 def dot(a, b, ca, cb):
@@ -30,10 +32,9 @@
     ba_s, slot_s, rank_s, slot_v, rank_v, tok_h, cot_h, w_h, dn_h, up_h,
     val_o, tig_o, dmg_o, umg_o,
     tok, cotf, w, dnf, upf, dnb, upb, base, rsr, reqs, tagr, tag_v, bi_v, scale,
-    usend, urecv, dsend, drecv, gsend, grecv, hsend, hrecv, grads, hgrads,
+    umid, usend, urecv, dmid, dsend, drecv, grads, gsend, grecv, gmid, gpart, hgrads, hsend, hrecv, hmid, hpart,
     arp, arr, tot, scaled, lorav, valv, tigv, dacc, uacc, tag_s, bi_s,
-    in_sem, out_sem, ag_s, ag_r, rs_s, rs_r, ar_s, ar_r, tg_s, tg_r,
-    us_s, us_r, ds_s, ds_r, gs_s, gs_r, hs_s, hs_r, sm_sem,
+    in_sem, out_sem, ag_s, ag_r, rs_s, rs_r, ar_s, ar_r, row_s, row_r, line_s, line_r, sm_sem,
 ):
     d = lax.axis_index("dp")
     z = lax.axis_index("tensor")
@@ -50,27 +51,37 @@
 
     barrier = pltpu.get_barrier_semaphore()
 
-    def greet(i, carry):
-        pl.semaphore_signal(barrier, inc=1, device_id=((d + i) % DP, z), device_id_type=MESH)
-        return carry
-
-    lax.fori_loop(1, DP, greet, 0)
+    def at(px, py, pc):
+        return px * 8 + py * 2 + pc
+
+    def beyond(hf, k2):
+        ahead, core = k2 // 2, (c + k2 % 2) % 2
+        if hf == 0:
+            pos = (x + ahead) % 4
+            return pos * 2 + core, at(pos, y, core)
+        pos = (y + ahead) % 4
+        return pos * 2 + core, at(x, pos, core)
+
+    def greet(k2, carry):
+        for hf in (0, 1):
+            pl.semaphore_signal(barrier, inc=1, device_id=(beyond(hf, k2)[1], z), device_id_type=MESH)
+        return carry
+
     for to in (right, left):
         pl.semaphore_signal(barrier, inc=1, device_id=(d, to), device_id_type=MESH)
-
-    own3 = lax.broadcasted_iota(I32, (DP, 8, 128), 0)
-    own2 = lax.broadcasted_iota(I32, (DP, 128), 0)
+    lax.fori_loop(1, 8, greet, 0)
+
     pair2 = lax.broadcasted_iota(I32, (8, 128), 0)
     lane2 = lax.broadcasted_iota(I32, (8, 128), 1)
-    tags = jnp.zeros((DP, 8, 128), I32)
-    which = jnp.zeros((DP, 128), I32)
+    tags = jnp.zeros((8, 128), I32)
+    which = jnp.zeros((8, 128), I32)
     ranks = jnp.ones((8, 128), I32)
     for b in range(NB):
         a = ba_s[b]
         s = slot_s[a]
         o = s // OWN
-        tags = jnp.where(own3 == o, s - o * OWN + 1, tags)
-        which = jnp.where(own2 == o, b, which)
+        tags = jnp.where(lane2 == o, s - o * OWN + 1, tags)
+        which = jnp.where(lane2 == o, b, which)
         here = (pair2 == b // 2) & ((lane2 >= R) if b % 2 else (lane2 < R))
         ranks = jnp.where(here, rank_s[a], ranks)
     reqs[...] = tags
@@ -78,7 +89,7 @@
     scale[...] = R / (4.0 * ranks.astype(F32))
     cp_bi = pltpu.make_async_copy(bi_v, bi_s, sm_sem.at[0])
     cp_bi.start()
-    pl.semaphore_wait(barrier, DP + 1)
+    pl.semaphore_wait(barrier, 16)
 
     def ag(m, dirn):
         h, cc = m // NC, m % NC
@@ -102,69 +113,125 @@
 
     lax.fori_loop(0, DEPTH, ag_first, 0)
 
-    def xmsg(i, src, dst, ss, rs):
-        j = (i * 13) % DP
-        px, py, pc = (x + j // 8) % 4, (y + (j // 2) % 4) % 4, (c + j % 2) % 2
-        t = px * 8 + py * 2 + pc
-        return t, pltpu.make_async_remote_copy(
-            src_ref=src.at[t], dst_ref=dst.at[d], send_sem=ss.at[i], recv_sem=rs.at[i],
-            device_id=(t, z), device_id_type=MESH)
-
-    def x_recv(src, dst, ss, rs):
-        def go(i, carry):
-            xmsg(i, src, dst, ss, rs)[1].wait_recv()
+    along = (y, x)
+    across = (x, y)
+    me8 = tuple(q * 2 + c for q in across)
+
+    def owner(hf, p, q, core):
+        return at(q, p, core) if hf == 0 else at(p, q, core)
+
+    def row_copy(e, hf, k2, src, dst):
+        return pltpu.make_async_remote_copy(
+            src_ref=src, dst_ref=dst, send_sem=row_s.at[e, hf, k2], recv_sem=row_r.at[e, hf, k2],
+            device_id=(beyond(hf, k2)[1], z), device_id_type=MESH)
+
+    def line_copy(e, hf, k, src, dst):
+        to = at(x, (y + k) % 4, c) if hf == 0 else at((x + k) % 4, y, c)
+        return pltpu.make_async_remote_copy(
+            src_ref=src, dst_ref=dst, send_sem=line_s.at[e, hf, k], recv_sem=line_r.at[e, hf, k],
+            device_id=(to, z), device_id_type=MESH)
+
+    TAG, UP, DOWN, GRAD, HGRAD = 0, 1, 2, 3, 4
+
+    def row_msg(e, hf, k2):
+        if e == TAG:
+            return row_copy(e, hf, k2, reqs, tagr.at[hf, me8[hf]])
+        g = beyond(hf, k2)[0]
+        if e in (UP, DOWN):
+            src, dst = ((usend, urecv), (dsend, drecv))[e - UP]
+            return row_copy(e, hf, k2, src.at[hf, g], dst.at[hf, pl.ds(me8[hf] * 4, 4)])
+        src, dst = ((gsend, grecv), (hsend, hrecv))[e - GRAD]
+        return row_copy(e, hf, k2, src.at[hf, g], dst.at[hf, me8[hf]])
+
+    def line_msg(e, hf, k):
+        p = along[hf]
+        if e in (UP, DOWN):
+            src, dst = ((upb, umid), (dnb, dmid))[e - UP]
+            return line_copy(e, hf, k, src.at[hf], dst.at[hf, p])
+        src, dst = ((gmid, gpart), (hmid, hpart))[e - GRAD]
+        return line_copy(e, hf, k, src.at[hf, (p + k) % 4], dst.at[hf, p])
+
+    def each_row(e, what):
+        def go(j, carry):
+            k2 = (j * 3) % 8
+            for hf in (0, 1):
+                what(row_msg(e, hf, k2), hf, k2)
             return carry
-        lax.fori_loop(1, DP, go, 0)
-
-    def x_sent(src, dst, ss, rs):
-        def go(i, carry):
-            xmsg(i, src, dst, ss, rs)[1].wait_send()
-            return carry
-        lax.fori_loop(1, DP, go, 0)
-
-    tg = (reqs, tagr, tg_s, tg_r)
-    us = (usend, urecv, us_s, us_r)
-    ds = (dsend, drecv, ds_s, ds_r)
-    gs = (gsend, grecv, gs_s, gs_r)
-    hs = (hsend, hrecv, hs_s, hs_r)
-
-    def tag_go(i, carry):
-        xmsg(i, *tg)[1].start()
-        return carry
-
-    lax.fori_loop(1, DP, tag_go, 0)
-    tagr[d] = reqs[d]
+        lax.fori_loop(1, 8, go, 0)
+
+    def each_line(e, what):
+        for k in (1, 3, 2):
+            for hf in (0, 1):
+                what(line_msg(e, hf, k))
+
+    def row_arrived(e):
+        each_row(e, lambda copy, hf, k2: copy.wait_recv())
+
+    def line_arrived(e):
+        each_line(e, lambda copy: copy.wait_recv())
+
+    each_row(TAG, lambda copy, hf, k2: copy.start())
+    for hf in (0, 1):
+        tagr[hf, me8[hf]] = reqs[...]
 
     cp_up.wait()
     cp_dn.wait()
+    RH = R // 2
     for l in range(OWN):
         mine = slot_v[...] == d * OWN + l
         rank = jnp.sum(jnp.where(mine, rank_v[...], 0), axis=1, keepdims=True)
-        upb[l] = jnp.where(lax.broadcasted_iota(I32, (R, HEAD), 0) < rank, upf[l], 0.0).astype(BF)
-        dnb[l] = jnp.where(lax.broadcasted_iota(I32, (R, FEAT), 0) < rank, dnf[l], 0.0).astype(BF)
-    x_recv(*tg)
-    tag_v[...] = tagr[:, 0, :]
+        for hf in (0, 1):
+            rows = slice(hf * RH, (hf + 1) * RH)
+            keep = lax.broadcasted_iota(I32, (RH, HEAD), 0) + hf * RH < rank
+            upb[hf, l] = jnp.where(keep, upf[l, rows, :], 0.0).astype(BF)
+    each_line(UP, lambda copy: copy.start())
+    for l in range(OWN):
+        mine = slot_v[...] == d * OWN + l
+        rank = jnp.sum(jnp.where(mine, rank_v[...], 0), axis=1, keepdims=True)
+        for hf in (0, 1):
+            rows = slice(hf * RH, (hf + 1) * RH)
+            keep = lax.broadcasted_iota(I32, (RH, FEAT), 0) + hf * RH < rank
+            dnb[hf, l] = jnp.where(keep, dnf[l, rows, :], 0.0).astype(BF)
+    each_line(DOWN, lambda copy: copy.start())
+    for hf in (0, 1):
+        umid[hf, along[hf]] = upb[hf]
+        dmid[hf, along[hf]] = dnb[hf]
+    row_arrived(TAG)
+    for hf in (0, 1):
+        tag_v[hf] = tagr[hf, :, 0, :]
     cp_tag = pltpu.make_async_copy(tag_v, tag_s, sm_sem.at[1])
     cp_tag.start()
     cp_tag.wait()
 
-    def fill(src, args):
-        def go(i, carry):
-            t, copy = xmsg(i, *args)
-            args[0][t] = src[jnp.maximum(tag_s[t, 0] - 1, 0)]
+    def wanted(hf, g, p):
+        return tag_s[hf, g, owner(hf, p, across[hf], c)]
+
+    def hand_on(e, mid, send, recv):
+        line_arrived(e)
+
+        def go(copy, hf, k2):
+            g = beyond(hf, k2)[0]
+            for p in range(4):
+                send[hf, g, p] = mid[hf, p, jnp.maximum(wanted(hf, g, p) - 1, 0)]
             copy.start()
-            return carry
-        lax.fori_loop(1, DP, go, 0)
-        args[1][d] = src[jnp.maximum(tag_s[d, 0] - 1, 0)]
-
-    fill(upb, us)
-    fill(dnb, ds)
+
+        each_row(e, go)
+        for hf in (0, 1):
+            for p in range(4):
+                recv[hf, me8[hf] * 4 + p] = mid[hf, p, jnp.maximum(wanted(hf, me8[hf], p) - 1, 0)]
+
+    hand_on(UP, umid, usend, urecv)
     cp_bi.wait()
     cp_tok.wait()
     cp_w.wait()
 
-    def owner_of(b):
-        return slot_s[ba_s[b]] // OWN
+    def of_block(recv, b):
+        o = slot_s[ba_s[b]] // OWN
+        ox, oy, oc = o // 8, (o // 2) % 4, o % 2
+        return [recv[0, (ox * 2 + oc) * 4 + oy], recv[1, (oy * 2 + oc) * 4 + ox]]
+
+    def of_blocks(recv, *bs):
+        return jnp.concatenate([part for b in bs for part in of_block(recv, b)], axis=0)
 
     half = (slice(0, BLK // 2), slice(BLK // 2, BLK))
 
@@ -215,40 +282,66 @@
     def rows_of(b, n=BLK):
         return pl.ds(pl.multiple_of(b * n, n), n)
 
-    def back_partial():
-        x_recv(*us)
+    def low_rank(e, q, recv, data):
+        row_arrived(e)
 
         def go(j, carry):
-            parts = []
-            for k in (0, 1):
-                b = 2 * j + k
-                parts.append(dot(cotf[z, rows_of(b), :], urecv[owner_of(b)], 1, 1))
-            arp[0, j] = jnp.concatenate(parts, axis=1).astype(BF)
+            parts = [dot(data(2 * j + k), of_blocks(recv, 2 * j + k), 1, 1) for k in (0, 1)]
+            arp[q, j] = jnp.concatenate(parts, axis=1).astype(BF)
             return carry
 
         lax.fori_loop(0, NZ, go, 0)
 
-    def low_partial():
-        x_recv(*ds)
-
-        def go(j, carry):
-            parts = []
-            for k in (0, 1):
-                b = 2 * j + k
-                parts.append(dot(tok[rows_of(b), :], drecv[owner_of(b)], 1, 1))
-            arp[1, j] = jnp.concatenate(parts, axis=1).astype(BF)
-            return carry
-
-        lax.fori_loop(0, NZ, go, 0)
-
-    def send_grads(src, args):
-        def go(i, carry):
-            t, copy = xmsg(i, *args)
-            args[0][t] = src[bi_s[t, 0]]
+    def tok_of(b):
+        return tok[rows_of(b), :]
+
+    def cot_of(b):
+        return cotf[z, rows_of(b), :]
+
+    def send_grads(e, src, send, recv):
+        def pick(hf, q, core, p):
+            return src[hf, bi_s[0, owner(hf, p, q, core)]]
+
+        def go(copy, hf, k2):
+            g = beyond(hf, k2)[0]
+            for p in range(4):
+                send[hf, g, p] = pick(hf, g // 2, g % 2, p)
             copy.start()
-            return carry
-        lax.fori_loop(1, DP, go, 0)
-        args[1][d] = src[bi_s[d, 0]]
+
+        each_row(e, go)
+        for hf in (0, 1):
+            for p in range(4):
+                recv[hf, me8[hf], p] = pick(hf, across[hf], c, p)
+
+    def tally(e, recv, mid, part, rows, width):
+        row_arrived(e)
+        for hf in (0, 1):
+            def tile(i, carry):
+                p, r = i // (RH // rows), i % (RH // rows)
+                here = pl.ds(pl.multiple_of(r * rows, rows), rows)
+
+                def add(g, sums):
+                    tag = wanted(hf, g, p)
+                    piece = recv[hf, g, p, here, :].astype(F32)
+                    return tuple(
+                        sums[l] + jnp.where(tag == l + 1, piece, 0.0) for l in range(OWN))
+
+                zero = jnp.zeros((rows, width), F32)
+                sums = lax.fori_loop(0, 8, add, (zero,) * OWN)
+                for l in range(OWN):
+                    mid[hf, p, l, here, :] = sums[l].astype(BF)
+                return carry
+            lax.fori_loop(0, 4 * (RH // rows), tile, 0)
+        each_line(e, lambda copy: copy.start())
+        for hf in (0, 1):
+            part[hf, along[hf]] = mid[hf, along[hf]]
+
+    def total(e, part, acc):
+        line_arrived(e)
+        for hf in (0, 1):
+            rows = slice(hf * RH, (hf + 1) * RH)
+            for l in range(OWN):
+                acc[l, rows, :] = sum(part[hf, p, l].astype(F32) for p in range(4))
 
     def down_grads():
         scale_all(0)
@@ -257,11 +350,13 @@
             turned = jnp.transpose(scaled[0, j].astype(F32)).astype(BF)
             for k in (0, 1):
                 b = 2 * j + k
-                grads[b] = dot(turned[k * R:(k + 1) * R], tok[rows_of(b), :], 1, 0).astype(BF)
+                piece = dot(turned[k * R:(k + 1) * R], tok_of(b), 1, 0).astype(BF)
+                for hf in (0, 1):
+                    grads[hf, b] = piece[hf * RH:(hf + 1) * RH]
             return carry
 
         lax.fori_loop(0, NZ, go, 0)
-        send_grads(grads, gs)
+        send_grads(GRAD, grads, gsend, grecv)
 
     def up_grads():
         scale_all(1)
@@ -269,16 +364,18 @@
         def go(j, carry):
             mine = scaled[1, j]
             turned = jnp.transpose(mine.astype(F32)).astype(BF)
-            ups = jnp.concatenate([urecv[owner_of(2 * j)], urecv[owner_of(2 * j + 1)]], axis=0)
+            ups = of_blocks(urecv, 2 * j, 2 * j + 1)
             for k in (0, 1):
                 b = 2 * j + k
-                hgrads[b] = dot(turned[k * R:(k + 1) * R], cotf[z, rows_of(b), :], 1, 0).astype(BF)
+                piece = dot(turned[k * R:(k + 1) * R], cot_of(b), 1, 0).astype(BF)
+                for hf in (0, 1):
+                    hgrads[hf, b] = piece[hf * RH:(hf + 1) * RH]
                 only = jnp.where((lanes >= R) if k else (lanes < R), mine, jnp.zeros((), BF))
                 lorav[rows_of(b), :] = dot(only, ups, 1, 0).astype(BF)
             return carry
 
         lax.fori_loop(0, NZ, go, 0)
-        send_grads(hgrads, hs)
+        send_grads(HGRAD, hgrads, hsend, hrecv)
 
     def base_chunk(cc):
         rows = rows_of(cc, CH)
@@ -295,10 +392,9 @@
         full = jnp.concatenate([cotf[k, rows, :] for k in range(NZ)], axis=1)
         part = dot(full, w[...], 1, 1)
         mine = scaled[0, cc]
-        dns = jnp.concatenate([drecv[owner_of(2 * cc)], drecv[owner_of(2 * cc + 1)]], axis=0)
         zero = jnp.zeros((), BF)
         both = jnp.concatenate([jnp.where(lanes < R, mine, zero), jnp.where(lanes >= R, mine, zero)], axis=0)
-        lora = dot(both, dns, 1, 0).astype(BF).astype(F32)
+        lora = dot(both, of_blocks(drecv, 2 * cc, 2 * cc + 1), 1, 0).astype(BF).astype(F32)
         tigv[rows, :] = (part + lora).astype(BF)
         tig_out(cc).start()
 
@@ -355,13 +451,17 @@
 
         @pl.when(t == T_UP)
         def _():
-            back_partial()
+            low_rank(UP, 0, urecv, cot_of)
 
         for k in range(8):
             @pl.when(t == T_BACK + k)
             def _():
                 ar_step(0, k)
 
+        @pl.when(t == T_HAND)
+        def _():
+            hand_on(DOWN, dmid, dsend, drecv)
+
         @pl.when(t >= LAST - NC)
         def _():
             base_chunk(t - (LAST - NC))
@@ -386,7 +486,7 @@
 
         @pl.when(t == T_DOWN)
         def _():
-            low_partial()
+            low_rank(DOWN, 1, drecv, tok_of)
 
         for k in range(9):
             @pl.when(t == T_LOW + k)
@@ -397,9 +497,17 @@
         def _():
             tig_chunk(t - T_DOWN - 1)
 
+        @pl.when(t == T_TALLY)
+        def _():
+            tally(GRAD, grecv, gmid, gpart, 16, FEAT)
+
         @pl.when(t == T_LOW + 8)
         def _():
             up_grads()
+
+        @pl.when(t == T_LOW + 10)
+        def _():
+            tally(HGRAD, hrecv, hmid, hpart, 32, HEAD)
         return carry
 
     lax.fori_loop(LAST, 2 * LAST, tick_b, 0)
@@ -413,33 +521,13 @@
         valv[rows, :] = (whole + lorav[rows, :].astype(F32)).astype(BF)
         return carry
 
+    total(GRAD, gpart, dacc)
+    cp_dm = pltpu.make_async_copy(dacc, dmg_o, out_sem.at[NC + 1])
+    cp_dm.start()
     lax.fori_loop(0, NC, finish, 0)
     cp_val = pltpu.make_async_copy(valv, val_o, out_sem.at[NC])
     cp_val.start()
-
-    def tally(recv, acc, rows, width):
-        def tile(r, carry):
-            here = pl.ds(pl.multiple_of(r * rows, rows), rows)
-
-            def add(s, sums):
-                tag = tag_s[s, 0]
-                piece = recv[s, here, :].astype(F32)
-                return tuple(
-                    sums[l] + jnp.where(tag == l + 1, piece, 0.0) for l in range(OWN))
-
-            zero = jnp.zeros((rows, width), F32)
-            sums = lax.fori_loop(0, DP, add, (zero,) * OWN)
-            for l in range(OWN):
-                acc[l, here, :] = sums[l]
-            return carry
-        lax.fori_loop(0, R // rows, tile, 0)
-
-    x_recv(*gs)
-    tally(grecv, dacc, 16, FEAT)
-    cp_dm = pltpu.make_async_copy(dacc, dmg_o, out_sem.at[NC + 1])
-    cp_dm.start()
-    x_recv(*hs)
-    tally(hrecv, uacc, 64, HEAD)
+    total(HGRAD, hpart, uacc)
     cp_um = pltpu.make_async_copy(uacc, umg_o, out_sem.at[NC + 2])
     cp_um.start()
 
@@ -449,8 +537,10 @@
         return carry
 
     lax.fori_loop(MSG - DEPTH, MSG, rs_rest, 0)
-    for args in (tg, us, ds, gs, hs):
-        x_sent(*args)
+    for e in (TAG, UP, DOWN, GRAD, HGRAD):
+        each_row(e, lambda copy, hf, k2: copy.wait_send())
+        if e != TAG:
+            each_line(e, lambda copy: copy.wait_send())
     for q in (0, 1):
         for k in range(8):
             for dirn in (0, 1):
@@ -471,25 +561,26 @@
     smem = pl.BlockSpec(memory_space=pltpu.SMEM)
     vmem = pl.BlockSpec(memory_space=pltpu.VMEM)
     hbm = pl.BlockSpec(memory_space=pl.ANY)
+    rh = R // 2
     scratch = [
         vm((ROWS, FEAT), BF), vm((NZ, ROWS, HEAD), BF), vm((FEAT, NZ * HEAD), BF),
-        vm((OWN, R, FEAT), F32), vm((OWN, R, HEAD), F32), vm((OWN, R, FEAT), BF), vm((OWN, R, HEAD), BF),
+        vm((OWN, R, FEAT), F32), vm((OWN, R, HEAD), F32), vm((2, OWN, rh, FEAT), BF), vm((2, OWN, rh, HEAD), BF),
         vm((NZ, ROWS, HEAD), BF), vm((2, MSG, CH, HEAD), BF),
-        vm((DP, 8, 128), I32), vm((DP, 8, 128), I32), vm((DP, 128), I32), vm((DP, 128), I32), vm((8, 128), F32),
-        vm((DP, R, HEAD), BF), vm((DP, R, HEAD), BF),
-        vm((DP, R, FEAT), BF), vm((DP, R, FEAT), BF),
-        vm((DP, R, FEAT), BF), vm((DP, R, FEAT), BF),
-        vm((DP, R, HEAD), BF), vm((DP, R, HEAD), BF),
-        vm((NB, R, FEAT), BF), vm((NB, R, HEAD), BF),
+        vm((8, 128), I32), vm((2, 8, 8, 128), I32), vm((2, 8, 128), I32), vm((8, 128), I32), vm((8, 128), F32),
+        vm((2, 4, OWN, rh, HEAD), BF), vm((2, 8, 4, rh, HEAD), BF), vm((2, DP, rh, HEAD), BF),
+        vm((2, 4, OWN, rh, FEAT), BF), vm((2, 8, 4, rh, FEAT), BF), vm((2, DP, rh, FEAT), BF),
+        vm((2, NB, rh, FEAT), BF), vm((2, 8, 4, rh, FEAT), BF), vm((2, 8, 4, rh, FEAT), BF),
+        vm((2, 4, OWN, rh, FEAT), BF), vm((2, 4, OWN, rh, FEAT), BF),
+        vm((2, NB, rh, HEAD), BF), vm((2, 8, 4, rh, HEAD), BF), vm((2, 8, 4, rh, HEAD), BF),
+        vm((2, 4, OWN, rh, HEAD), BF), vm((2, 4, OWN, rh, HEAD), BF),
         vm((2, NZ, BLK, 2 * R), BF), vm((2, 2, 4, BLK, 2 * R), BF), vm((2, NZ, BLK, 2 * R), BF), vm((2, NZ, BLK, 2 * R), BF),
         vm((ROWS, HEAD), BF), vm((ROWS, HEAD), BF), vm((ROWS, FEAT), BF),
         vm((OWN, R, FEAT), F32), vm((OWN, R, HEAD), F32),
-        pltpu.SMEM((DP, 128), I32), pltpu.SMEM((DP, 128), I32),
+        pltpu.SMEM((2, 8, 128), I32), pltpu.SMEM((8, 128), I32),
         dma((5,)), dma((NC + 3,)),
         dma((2, MSG)), dma((2, MSG)), dma((2, MSG)), dma((2, MSG)),
         dma((2, 2, 8)), dma((2, 2, 8)),
-        dma((DP,)), dma((DP,)), dma((DP,)), dma((DP,)), dma((DP,)), dma((DP,)),
-        dma((DP,)), dma((DP,)), dma((DP,)), dma((DP,)), dma((2,)),
+        dma((5, 2, 8)), dma((5, 2, 8)), dma((5, 2, 4)), dma((5, 2, 4)), dma((2,)),
     ]
     val, tig, dmg, umg = pl.pallas_call(
         kernel,

time: 140 us -> 131 us (0.936); the launches traced: 139 us -> 128 us
  Pallas kernels: 132 us -> 121 us
    pallas_call x1, Pallas kernels: 132 us -> 121 us  [on_device(): pl.pallas_call(kernel, out_shape=(jax.ShapeDtypeStruct((ROWS, HEAD), BF),...]
where the time goes in v2:
time: 131 us; the launch traced here: 128 us
  Pallas kernels  121 us (92%)
  local copies, waits for them, and re-layouts  6.9 us (5%)
    pallas_call x1, Pallas kernels, on_device(): pl.pallas_call(kernel, out_shape=(jax.ShapeDtypeStruct((ROWS, HEAD), BF),...  121 us
    unnamed x8, local copies, waits for them, and re-layouts  6.9 us

profile of v2, /device:TPU:6, one launch (start us, length us, event | category | flops | bytes accessed | tf_op | source)
XLA Modules:
  0.0 128.3 jit_solution(8043970381927133027)
XLA Ops:
  0.6 120.8 %shard_map.111 = (bf16[2048,128]{1,0:T(8,128)(2,1)}, bf16[2048,640]{1,0:T(8,128)(2,1)}, f32[4,64,640]{2,1,0:T(8,128)}, f32[4,64,128]{2,1,0:T(8,128)}) custom-call(s32[16]{0:T(128)} %ba_s.1, s32[128]{0:T(128)} %slot_s.1, s32[128]{0:T(128)} %rank_s.1, s32[1,128]{1,0:T(1,128)} %bitcast.6, s32[1,128]{1,0:T(1,128)} %bitcast.7, bf16[2048,640]{1,0:T(8,128)(2,1)} %tok_h.1, ...), custom_call_target="tpu_custom_call" | custom-call | tf_op jit(solution)/shard_map/pallas_call | solution.py:585
  121.4 1.9 %copy.16 = bf16[2048,128]{1,0:T(8,128)(2,1)} copy(bf16[2048,128]{1,0:T(8,128)(2,1)} %get-tuple-element.16) | data formatting | bytes 1048576
  123.3 0.0 copy-start
  123.3 0.0 copy-start.1
  123.3 3.5 %copy.17 = bf16[2048,640]{1,0:T(8,128)(2,1)} copy(bf16[2048,640]{1,0:T(8,128)(2,1)} %get-tuple-element.17) | data formatting | bytes 5242880
  126.8 0.0 copy-done
  126.8 0.8 copy.18
  127.6 0.0 copy-done.1
  127.6 0.7 copy.19
Async XLA Ops:
  123.3 3.5 %copy-start = (f32[4,64,640]{2,1,0:T(8,128)S(1)}, f32[4,64,640]{2,1,0:T(8,128)}, u32[]{:S(2)}) copy-start(f32[4,64,640]{2,1,0:T(8,128)} %get-tuple-element.10) | copy-start | bytes 1966084
  123.3 4.4 %copy-start.1 = (f32[4,64,128]{2,1,0:T(8,128)S(1)}, f32[4,64,128]{2,1,0:T(8,128)}, u32[]{:S(2)}) copy-start(f32[4,64,128]{2,1,0:T(8,128)} %get-tuple-element.19) | copy-start | bytes 393220

commit v3 on v2

--- a/solution.py
+++ b/solution.py
@@ -14,14 +14,19 @@
 CH = 256
 NC = ROWS // CH
 MSG = 3 * NC + NC // 2
-DEPTH = 4
-LAST = MSG // 2
-T_UP = 5
-T_BACK = T_UP + 1
-T_HAND = 6
-T_DOWN = 15
-T_LOW = T_DOWN + 1
-T_TALLY = 22
+DEPTH = 3
+U_BACK = 8
+U_HAND = 11
+U_LOW = 24
+HOPS = (3, 3)
+U_BACK_HOP = U_BACK + 1
+U_LOW_HOP = U_LOW + 2
+U_BACK_END = U_BACK_HOP + 8 * HOPS[0]
+U_LOW_END = U_LOW_HOP + 8 * HOPS[1]
+U_BASE = 9
+U_TIG = U_BACK_END + 2
+U_TALLY = 46
+U_HTALLY = U_LOW_END + 4
 
 
 def dot(a, b, ca, cb):
@@ -30,11 +35,11 @@
 
 def kernel(
     ba_s, slot_s, rank_s, slot_v, rank_v, tok_h, cot_h, w_h, dn_h, up_h,
-    val_o, tig_o, dmg_o, umg_o,
+    valv, tigv, dacc, uacc,
     tok, cotf, w, dnf, upf, dnb, upb, base, rsr, reqs, tagr, tag_v, bi_v, scale,
     umid, usend, urecv, dmid, dsend, drecv, grads, gsend, grecv, gmid, gpart, hgrads, hsend, hrecv, hmid, hpart,
-    arp, arr, tot, scaled, lorav, valv, tigv, dacc, uacc, tag_s, bi_s,
-    in_sem, out_sem, ag_s, ag_r, rs_s, rs_r, ar_s, ar_r, row_s, row_r, line_s, line_r, sm_sem,
+    arp, arr, tot, scaled, lorav, tag_s, bi_s,
+    in_sem, ag_s, ag_r, rs_s, rs_r, ar_s, ar_r, row_s, row_r, line_s, line_r, sm_sem,
 ):
     d = lax.axis_index("dp")
     z = lax.axis_index("tensor")
@@ -192,7 +197,6 @@
             rows = slice(hf * RH, (hf + 1) * RH)
             keep = lax.broadcasted_iota(I32, (RH, FEAT), 0) + hf * RH < rank
             dnb[hf, l] = jnp.where(keep, dnf[l, rows, :], 0.0).astype(BF)
-    each_line(DOWN, lambda copy: copy.start())
     for hf in (0, 1):
         umid[hf, along[hf]] = upb[hf]
         dmid[hf, along[hf]] = dnb[hf]
@@ -221,6 +225,7 @@
                 recv[hf, me8[hf] * 4 + p] = mid[hf, p, jnp.maximum(wanted(hf, me8[hf], p) - 1, 0)]
 
     hand_on(UP, umid, usend, urecv)
+    each_line(DOWN, lambda copy: copy.start())
     cp_bi.wait()
     cp_tok.wait()
     cp_w.wait()
@@ -282,15 +287,13 @@
     def rows_of(b, n=BLK):
         return pl.ds(pl.multiple_of(b * n, n), n)
 
-    def low_rank(e, q, recv, data):
-        row_arrived(e)
-
+    def low_rank(q, recv, data, lo, hi):
         def go(j, carry):
             parts = [dot(data(2 * j + k), of_blocks(recv, 2 * j + k), 1, 1) for k in (0, 1)]
             arp[q, j] = jnp.concatenate(parts, axis=1).astype(BF)
             return carry
 
-        lax.fori_loop(0, NZ, go, 0)
+        lax.fori_loop(lo, hi, go, 0)
 
     def tok_of(b):
         return tok[rows_of(b), :]
@@ -313,27 +316,25 @@
             for p in range(4):
                 recv[hf, me8[hf], p] = pick(hf, across[hf], c, p)
 
-    def tally(e, recv, mid, part, rows, width):
-        row_arrived(e)
-        for hf in (0, 1):
-            def tile(i, carry):
-                p, r = i // (RH // rows), i % (RH // rows)
-                here = pl.ds(pl.multiple_of(r * rows, rows), rows)
-
-                def add(g, sums):
-                    tag = wanted(hf, g, p)
-                    piece = recv[hf, g, p, here, :].astype(F32)
-                    return tuple(
-                        sums[l] + jnp.where(tag == l + 1, piece, 0.0) for l in range(OWN))
-
-                zero = jnp.zeros((rows, width), F32)
-                sums = lax.fori_loop(0, 8, add, (zero,) * OWN)
+    def tally(e, recv, mid, part, halves=(0, 1)):
+        shape = (OWN * RH, 8 * RH)
+        to, frm = lax.broadcasted_iota(I32, shape, 0), lax.broadcasted_iota(I32, shape, 1)
+        same_row = (to % RH) == (frm % RH)
+        slot, core = to // RH + 1, frm // RH
+        for hf in halves:
+            def place(p, carry):
+                tags = jnp.zeros(shape, I32)
+                for g in range(8):
+                    tags = jnp.where(core == g, wanted(hf, g, p), tags)
+                pick = jnp.where(same_row & (tags == slot), 1.0, 0.0).astype(BF)
+                pieces = jnp.concatenate([recv[hf, g, p] for g in range(8)], axis=0)
+                sums = dot(pick, pieces, 1, 0).astype(BF)
                 for l in range(OWN):
-                    mid[hf, p, l, here, :] = sums[l].astype(BF)
+                    mid[hf, p, l] = sums[l * RH:(l + 1) * RH]
                 return carry
-            lax.fori_loop(0, 4 * (RH // rows), tile, 0)
-        each_line(e, lambda copy: copy.start())
-        for hf in (0, 1):
+            lax.fori_loop(0, 4, place, 0)
+            for k in (1, 3, 2):
+                line_msg(e, hf, k).start()
             part[hf, along[hf]] = mid[hf, along[hf]]
 
     def total(e, part, acc):
@@ -356,7 +357,6 @@
             return carry
 
         lax.fori_loop(0, NZ, go, 0)
-        send_grads(GRAD, grads, gsend, grecv)
 
     def up_grads():
         scale_all(1)
@@ -364,18 +364,26 @@
         def go(j, carry):
             mine = scaled[1, j]
             turned = jnp.transpose(mine.astype(F32)).astype(BF)
-            ups = of_blocks(urecv, 2 * j, 2 * j + 1)
             for k in (0, 1):
                 b = 2 * j + k
                 piece = dot(turned[k * R:(k + 1) * R], cot_of(b), 1, 0).astype(BF)
                 for hf in (0, 1):
                     hgrads[hf, b] = piece[hf * RH:(hf + 1) * RH]
-                only = jnp.where((lanes >= R) if k else (lanes < R), mine, jnp.zeros((), BF))
-                lorav[rows_of(b), :] = dot(only, ups, 1, 0).astype(BF)
             return carry
 
         lax.fori_loop(0, NZ, go, 0)
-        send_grads(HGRAD, hgrads, hsend, hrecv)
+
+    def apart(mine):
+        zero = jnp.zeros((), BF)
+        return jnp.concatenate([jnp.where(lanes < R, mine, zero), jnp.where(lanes >= R, mine, zero)], axis=0)
+
+    def lora_values():
+        def go(j, carry):
+            ups = of_blocks(urecv, 2 * j, 2 * j + 1)
+            lorav[rows_of(j, CH), :] = dot(apart(scaled[1, j]), ups, 1, 0).astype(BF)
+            return carry
+
+        lax.fori_loop(0, NZ, go, 0)
 
     def base_chunk(cc):
         rows = rows_of(cc, CH)
@@ -383,20 +391,12 @@
         for k in range(NZ):
             base[k, rows, :] = part[:, k * HEAD:(k + 1) * HEAD].astype(BF)
 
-    def tig_out(cc):
-        rows = rows_of(cc, CH)
-        return pltpu.make_async_copy(tigv.at[rows], tig_o.at[rows], out_sem.at[cc])
-
     def tig_chunk(cc):
         rows = rows_of(cc, CH)
         full = jnp.concatenate([cotf[k, rows, :] for k in range(NZ)], axis=1)
         part = dot(full, w[...], 1, 1)
-        mine = scaled[0, cc]
-        zero = jnp.zeros((), BF)
-        both = jnp.concatenate([jnp.where(lanes < R, mine, zero), jnp.where(lanes >= R, mine, zero)], axis=0)
-        lora = dot(both, of_blocks(drecv, 2 * cc, 2 * cc + 1), 1, 0).astype(BF).astype(F32)
+        lora = dot(apart(scaled[0, cc]), of_blocks(drecv, 2 * cc, 2 * cc + 1), 1, 0).astype(BF).astype(F32)
         tigv[rows, :] = (part + lora).astype(BF)
-        tig_out(cc).start()
 
     def rs(n, h, cc, dirn):
         rows = rows_of(cc, CH)
@@ -425,10 +425,19 @@
             ag(m, dirn).start()
 
     def rs_step(n):
+        @pl.when(n < DEPTH)
+        def _():
+            for dirn in (0, 1):
+                ag(MSG - DEPTH + n, dirn).wait_send()
+
+        @pl.when(n >= DEPTH)
+        def _():
+            for dirn in (0, 1):
+                rs(n - DEPTH, 3, 0, dirn).wait_send()
+
         @pl.when(n < 4)
         def _():
             for dirn in (0, 1):
-                ag(MSG - DEPTH + n, dirn).wait_send()
                 rs(n, 4, n + dirn * 4, dirn).start()
 
         @pl.when(n >= 4)
@@ -442,75 +451,66 @@
                 @pl.when(k > 0)
                 def _():
                     rs_add(n - NC, 3 - k, cc, dirn)
-                rs(n - DEPTH, 3, cc, dirn).wait_send()
                 rs(n, 3 - k, cc, dirn).start()
-
-    def tick_a(t, carry):
-        ag_step(2 * t)
-        ag_step(2 * t + 1)
-
-        @pl.when(t == T_UP)
-        def _():
-            low_rank(UP, 0, urecv, cot_of)
-
-        for k in range(8):
-            @pl.when(t == T_BACK + k)
-            def _():
-                ar_step(0, k)
-
-        @pl.when(t == T_HAND)
-        def _():
-            hand_on(DOWN, dmid, dsend, drecv)
-
-        @pl.when(t >= LAST - NC)
-        def _():
-            base_chunk(t - (LAST - NC))
-        return carry
-
-    lax.fori_loop(DEPTH // 2, LAST, tick_a, 0)
-    ar_step(0, 8)
-    down_grads()
 
     def ag_rest(m, carry):
         ag(m, 0).wait_recv()
         ag(m - NC // 2 + (m // (3 * NC)) * (NC // 2), 1).wait_recv()
         return carry
 
-    def tick_b(t, carry):
-        rs_step(2 * (t - LAST))
-        rs_step(2 * (t - LAST) + 1)
-
-        @pl.when(t == LAST + 1)
+    def every(u, first, step, n, what):
+        @pl.when((u >= first) & (u < first + n * step) & ((u - first) % step == 0))
         def _():
-            lax.fori_loop(MSG - NC, MSG, ag_rest, 0)
-
-        @pl.when(t == T_DOWN)
-        def _():
-            low_rank(DOWN, 1, drecv, tok_of)
-
+            what((u - first) // step)
+
+    def hops(u, first, q, lo, hi):
         for k in range(9):
-            @pl.when(t == T_LOW + k)
-            def _():
-                ar_step(1, k)
-
-        @pl.when((t > T_DOWN) & (t <= T_DOWN + NC))
-        def _():
-            tig_chunk(t - T_DOWN - 1)
-
-        @pl.when(t == T_TALLY)
-        def _():
-            tally(GRAD, grecv, gmid, gpart, 16, FEAT)
-
-        @pl.when(t == T_LOW + 8)
-        def _():
-            up_grads()
-
-        @pl.when(t == T_LOW + 10)
-        def _():
-            tally(HGRAD, hrecv, hmid, hpart, 32, HEAD)
-        return carry
-
-    lax.fori_loop(LAST, 2 * LAST, tick_b, 0)
+            if lo <= first + k * HOPS[q] < hi:
+                @pl.when(u == first + k * HOPS[q])
+                def _():
+                    ar_step(q, k)
+
+    def run(lo, hi, step):
+        def at_slot(first, what, *args):
+            if lo <= first < hi:
+                @pl.when(u_now[0] == first)
+                def _():
+                    what(*args)
+
+        u_now = [None]
+
+        def slot(u, carry):
+            u_now[0] = u
+            step(u)
+            at_slot(U_BACK, row_arrived, UP)
+            at_slot(U_BACK, low_rank, 0, urecv, cot_of, 0, NZ)
+            at_slot(U_HAND, hand_on, DOWN, dmid, dsend, drecv)
+            at_slot(U_LOW, row_arrived, DOWN)
+            at_slot(U_LOW, low_rank, 1, drecv, tok_of, 0, NZ // 2)
+            at_slot(U_LOW + 1, low_rank, 1, drecv, tok_of, NZ // 2, NZ)
+            hops(u, U_BACK_HOP, 0, lo, hi)
+            hops(u, U_LOW_HOP, 1, lo, hi)
+            if lo < U_BASE + 2 * NC and U_BASE < hi:
+                every(u, U_BASE, 2, NC, base_chunk)
+            at_slot(U_BACK_END, down_grads)
+            at_slot(U_BACK_END + 1, send_grads, GRAD, grads, gsend, grecv)
+            at_slot(U_TIG, lax.fori_loop, MSG - NC, MSG, ag_rest, 0)
+            if lo < U_TIG + 2 * NC and U_TIG < hi:
+                every(u, U_TIG, 2, NC, tig_chunk)
+            at_slot(U_TALLY, row_arrived, GRAD)
+            at_slot(U_TALLY, tally, GRAD, grecv, gmid, gpart, (0,))
+            at_slot(U_TALLY + 1, tally, GRAD, grecv, gmid, gpart, (1,))
+            at_slot(U_LOW_END, up_grads)
+            at_slot(U_LOW_END + 1, send_grads, HGRAD, hgrads, hsend, hrecv)
+            at_slot(U_LOW_END + 2, lora_values)
+            at_slot(U_HTALLY, row_arrived, HGRAD)
+            at_slot(U_HTALLY, tally, HGRAD, hrecv, hmid, hpart)
+            return carry
+
+        lax.fori_loop(lo, hi, slot, 0)
+
+    run(DEPTH, MSG, ag_step)
+    run(MSG, 2 * MSG, lambda u: rs_step(u - MSG))
 
     def finish(cc, carry):
         n = MSG - NC + cc
@@ -522,14 +522,8 @@
         return carry
 
     total(GRAD, gpart, dacc)
-    cp_dm = pltpu.make_async_copy(dacc, dmg_o, out_sem.at[NC + 1])
-    cp_dm.start()
     lax.fori_loop(0, NC, finish, 0)
-    cp_val = pltpu.make_async_copy(valv, val_o, out_sem.at[NC])
-    cp_val.start()
     total(HGRAD, hpart, uacc)
-    cp_um = pltpu.make_async_copy(uacc, umg_o, out_sem.at[NC + 2])
-    cp_um.start()
 
     def rs_rest(n, carry):
         for dirn in (0, 1):
@@ -546,14 +540,14 @@
             for dirn in (0, 1):
                 ar_msg(q, k, dirn).wait_send()
 
-    def tig_rest(cc, carry):
-        tig_out(cc).wait()
-        return carry
-
-    lax.fori_loop(0, NC, tig_rest, 0)
-    cp_val.wait()
-    cp_dm.wait()
-    cp_um.wait()
+
+def hand_out(*refs):
+    n = len(refs) // 2
+    copies = [pltpu.make_async_copy(refs[i], refs[n + i], refs[-1].at[i]) for i in range(n)]
+    for copy in copies:
+        copy.start()
+    for copy in copies:
+        copy.wait()
 
 
 def on_device(tokens, cotangent, base_weight, adapter_down, adapter_up, block_adapter, adapter_slot, adapter_rank):
@@ -574,10 +568,9 @@
         vm((2, NB, rh, HEAD), BF), vm((2, 8, 4, rh, HEAD), BF), vm((2, 8, 4, rh, HEAD), BF),
         vm((2, 4, OWN, rh, HEAD), BF), vm((2, 4, OWN, rh, HEAD), BF),
         vm((2, NZ, BLK, 2 * R), BF), vm((2, 2, 4, BLK, 2 * R), BF), vm((2, NZ, BLK, 2 * R), BF), vm((2, NZ, BLK, 2 * R), BF),
-        vm((ROWS, HEAD), BF), vm((ROWS, HEAD), BF), vm((ROWS, FEAT), BF),
-        vm((OWN, R, FEAT), F32), vm((OWN, R, HEAD), F32),
+        vm((ROWS, HEAD), BF),
         pltpu.SMEM((2, 8, 128), I32), pltpu.SMEM((8, 128), I32),
-        dma((5,)), dma((NC + 3,)),
+        dma((5,)),
         dma((2, MSG)), dma((2, MSG)), dma((2, MSG)), dma((2, MSG)),
         dma((2, 2, 8)), dma((2, 2, 8)),
         dma((5, 2, 8)), dma((5, 2, 8)), dma((5, 2, 4)), dma((5, 2, 4)), dma((2,)),
@@ -585,13 +578,9 @@
     val, tig, dmg, umg = pl.pallas_call(
         kernel,
         out_shape=(
-            jax.ShapeDtypeStruct((ROWS, HEAD), BF),
-            jax.ShapeDtypeStruct((ROWS, FEAT), BF),
-            jax.ShapeDtypeStruct((OWN, R, FEAT), F32),
-            jax.ShapeDtypeStruct((OWN, R, HEAD), F32),
-        ),
+            vm((ROWS, HEAD), BF), vm((ROWS, FEAT), BF), vm((OWN, R, FEAT), F32), vm((OWN, R, HEAD), F32)),
         in_specs=[smem, smem, smem, vmem, vmem, hbm, hbm, hbm, hbm, hbm],
-        out_specs=(hbm, hbm, hbm, hbm),
+        out_specs=(vmem,) * 4,
         scratch_shapes=scratch,
         compiler_params=pltpu.CompilerParams(
             collective_id=0, has_side_effects=True, vmem_limit_bytes=54 * 2**20),
@@ -600,6 +589,15 @@
         adapter_slot.reshape(1, -1), adapter_rank.reshape(1, -1),
         tokens, cotangent, base_weight, jnp.swapaxes(adapter_down, 1, 2), adapter_up,
     )
+    outs = (val, tig, dmg, umg)
+    val, tig, dmg, umg = pl.pallas_call(
+        hand_out,
+        out_shape=tuple(jax.ShapeDtypeStruct(o.shape, o.dtype) for o in outs),
+        in_specs=[vmem] * 4,
+        out_specs=(hbm,) * 4,
+        scratch_shapes=[dma((4,))],
+        compiler_params=pltpu.CompilerParams(vmem_limit_bytes=4 * 2**20),
+    )(*outs)
     return val, tig, jnp.swapaxes(dmg, 1, 2), umg
 
 

time: 131 us -> 113 us (0.86)
  Pallas kernels: 121 us -> 110 us
  local copies, waits for them, and re-layouts: 6.9 us -> 0 us
    pallas_call x1 -> x2, Pallas kernels: 121 us -> 110 us  [the longest x1 108 us: on_device(): pl.pallas_call(kernel, out_shape=(vm((ROWS, HEAD), BF), vm((ROWS, FEAT),...]
    unnamed x8 -> x0, local copies, waits for them, and re-layouts: 6.9 us -> none
where the time goes in v3:
time: 113 us; the launch traced here: 111 us
  Pallas kernels  110 us (97%)
    pallas_call x1, Pallas kernels, on_device(): pl.pallas_call(kernel, out_shape=(vm((ROWS, HEAD), BF), vm((ROWS, FEAT),...  108 us

profile of v3, /device:TPU:6, one launch (start us, length us, event | category | flops | bytes accessed | tf_op | source)
XLA Modules:
  0.0 110.5 jit_solution(11803378903470971101)
XLA Ops:
  0.6 107.9 %shard_map.111 = (bf16[2048,128]{1,0:T(8,128)(2,1)S(1)}, bf16[2048,640]{1,0:T(8,128)(2,1)S(1)}, f32[4,64,640]{2,1,0:T(8,128)S(1)}, f32[4,64,128]{2,1,0:T(8,128)S(1)}) custom-call(s32[16]{0:T(128)} %ba_s.1, s32[128]{0:T(128)} %slot_s.1, s32[128]{0:T(128)} %rank_s.1, s32[1,128]{1,0:T(1,128)} %bitcast.5, s32[1,128]{1,0:T(1,128)} %bitcast.6, ...), custom_call_target="tpu_custom_call" | custom-call | tf_op jit(solution)/shard_map/pallas_call | solution.py:578
  108.6 1.9 %shard_map.112 = (bf16[2048,128]{1,0:T(8,128)(2,1)}, bf16[2048,640]{1,0:T(8,128)(2,1)}, f32[4,64,640]{2,1,0:T(8,128)}, f32[4,64,128]{2,1,0:T(8,128)}) custom-call(bf16[2048,128]{1,0:T(8,128)(2,1)S(1)} %get-tuple-element.12.refs_0_, bf16[2048,640]{1,0:T(8,128)(2,1)S(1)} %get-tuple-element.13.refs_1_, f32[4,64,640]{2,1,0:T(8,128)S(1)} %get-tuple-element.14.refs_2_, ...), custom_call_target="tpu_custom_call" | custom-call | tf_op jit(solution)/shard_map/pallas_call | solution.py:593

commit v4 on v3

--- a/solution.py
+++ b/solution.py
@@ -27,6 +27,7 @@
 U_TIG = U_BACK_END + 2
 U_TALLY = 46
 U_HTALLY = U_LOW_END + 4
+U_SENT = 30
 
 
 def dot(a, b, ca, cb):
@@ -174,6 +175,12 @@
 
     def line_arrived(e):
         each_line(e, lambda copy: copy.wait_recv())
+
+    def row_sent(e):
+        each_row(e, lambda copy, hf, k2: copy.wait_send())
+
+    def line_sent(e):
+        each_line(e, lambda copy: copy.wait_send())
 
     each_row(TAG, lambda copy, hf, k2: copy.start())
     for hf in (0, 1):
@@ -276,6 +283,11 @@
             for dirn in (0, 1):
                 ar_msg(q, k, dirn).start()
 
+    def ar_sent(q):
+        for k in range(8):
+            for dirn in (0, 1):
+                ar_msg(q, k, dirn).wait_send()
+
     def scale_all(q):
         def go(j, carry):
             scaled[q, j] = (scale[pl.ds(j, 1), :] * tot[q, j].astype(F32)).astype(BF)
@@ -503,6 +515,14 @@
             at_slot(U_LOW_END, up_grads)
             at_slot(U_LOW_END + 1, send_grads, HGRAD, hgrads, hsend, hrecv)
             at_slot(U_LOW_END + 2, lora_values)
+            at_slot(U_SENT, row_sent, TAG)
+            at_slot(U_SENT, line_sent, UP)
+            at_slot(U_SENT + 2, row_sent, UP)
+            at_slot(U_SENT + 4, line_sent, DOWN)
+            at_slot(U_SENT + 8, row_sent, DOWN)
+            at_slot(U_SENT + 10, ar_sent, 0)
+            at_slot(U_TALLY + 4, row_sent, GRAD)
+            at_slot(U_LOW_END + 3, ar_sent, 1)
             at_slot(U_HTALLY, row_arrived, HGRAD)
             at_slot(U_HTALLY, tally, HGRAD, hrecv, hmid, hpart)
             return carry
@@ -531,14 +551,9 @@
         return carry
 
     lax.fori_loop(MSG - DEPTH, MSG, rs_rest, 0)
-    for e in (TAG, UP, DOWN, GRAD, HGRAD):
-        each_row(e, lambda copy, hf, k2: copy.wait_send())
-        if e != TAG:
-            each_line(e, lambda copy: copy.wait_send())
-    for q in (0, 1):
-        for k in range(8):
-            for dirn in (0, 1):
-                ar_msg(q, k, dirn).wait_send()
+    for e in (GRAD, HGRAD):
+        line_sent(e)
+    row_sent(HGRAD)
 
 
 def hand_out(*refs):

time: 113 us -> 112 us (level)
  no operation moved by 1% of the time
where the time goes in v4:
time: 112 us; the launch traced here: 110 us
  Pallas kernels  110 us (98%)
    pallas_call x1, Pallas kernels, on_device(): pl.pallas_call(kernel, out_shape=(vm((ROWS, HEAD), BF), vm((ROWS, FEAT),...  108 us

profile of v4, /device:TPU:6, one launch (start us, length us, event | category | flops | bytes accessed | tf_op | source)
XLA Modules:
  0.0 110.2 jit_solution(11874979650399305403)
XLA Ops:
  0.6 107.6 %shard_map.111 = (bf16[2048,128]{1,0:T(8,128)(2,1)S(1)}, bf16[2048,640]{1,0:T(8,128)(2,1)S(1)}, f32[4,64,640]{2,1,0:T(8,128)S(1)}, f32[4,64,128]{2,1,0:T(8,128)S(1)}) custom-call(s32[16]{0:T(128)} %ba_s.1, s32[128]{0:T(128)} %slot_s.1, s32[128]{0:T(128)} %rank_s.1, s32[1,128]{1,0:T(1,128)} %bitcast.5, s32[1,128]{1,0:T(1,128)} %bitcast.6, ...), custom_call_target="tpu_custom_call" | custom-call | tf_op jit(solution)/shard_map/pallas_call | solution.py:593
  108.2 1.9 %shard_map.112 = (bf16[2048,128]{1,0:T(8,128)(2,1)}, bf16[2048,640]{1,0:T(8,128)(2,1)}, f32[4,64,640]{2,1,0:T(8,128)}, f32[4,64,128]{2,1,0:T(8,128)}) custom-call(bf16[2048,128]{1,0:T(8,128)(2,1)S(1)} %get-tuple-element.12.refs_0_, bf16[2048,640]{1,0:T(8,128)(2,1)S(1)} %get-tuple-element.13.refs_1_, f32[4,64,640]{2,1,0:T(8,128)S(1)} %get-tuple-element.14.refs_2_, ...), custom_call_target="tpu_custom_call" | custom-call | tf_op jit(solution)/shard_map/pallas_call | solution.py:608

commit v5 on v4

--- a/solution.py
+++ b/solution.py
@@ -14,7 +14,7 @@
 CH = 256
 NC = ROWS // CH
 MSG = 3 * NC + NC // 2
-DEPTH = 3
+DEPTH = 4
 U_BACK = 8
 U_HAND = 11
 U_LOW = 24
@@ -39,7 +39,7 @@
     valv, tigv, dacc, uacc,
     tok, cotf, w, dnf, upf, dnb, upb, base, rsr, reqs, tagr, tag_v, bi_v, scale,
     umid, usend, urecv, dmid, dsend, drecv, grads, gsend, grecv, gmid, gpart, hgrads, hsend, hrecv, hmid, hpart,
-    arp, arr, tot, scaled, lorav, tag_s, bi_s,
+    arp, arr, tot, scaled, lorav, picks, tag_s, bi_s,
     in_sem, ag_s, ag_r, rs_s, rs_r, ar_s, ar_r, row_s, row_r, line_s, line_r, sm_sem,
 ):
     d = lax.axis_index("dp")
@@ -328,19 +328,26 @@
             for p in range(4):
                 recv[hf, me8[hf], p] = pick(hf, across[hf], c, p)
 
-    def tally(e, recv, mid, part, halves=(0, 1)):
+    def choose(hf):
         shape = (OWN * RH, 8 * RH)
         to, frm = lax.broadcasted_iota(I32, shape, 0), lax.broadcasted_iota(I32, shape, 1)
         same_row = (to % RH) == (frm % RH)
         slot, core = to // RH + 1, frm // RH
+
+        def place(p, carry):
+            tags = jnp.zeros(shape, I32)
+            for g in range(8):
+                tags = jnp.where(core == g, wanted(hf, g, p), tags)
+            picks[hf, p] = jnp.where(same_row & (tags == slot), 1.0, 0.0).astype(BF)
+            return carry
+
+        lax.fori_loop(0, 4, place, 0)
+
+    def tally(e, recv, mid, part, halves=(0, 1)):
         for hf in halves:
             def place(p, carry):
-                tags = jnp.zeros(shape, I32)
-                for g in range(8):
-                    tags = jnp.where(core == g, wanted(hf, g, p), tags)
-                pick = jnp.where(same_row & (tags == slot), 1.0, 0.0).astype(BF)
                 pieces = jnp.concatenate([recv[hf, g, p] for g in range(8)], axis=0)
-                sums = dot(pick, pieces, 1, 0).astype(BF)
+                sums = dot(picks[hf, p], pieces, 1, 0).astype(BF)
                 for l in range(OWN):
                     mid[hf, p, l] = sums[l * RH:(l + 1) * RH]
                 return carry
@@ -493,6 +500,8 @@
 
         def slot(u, carry):
             u_now[0] = u
+            hops(u, U_BACK_HOP, 0, lo, hi)
+            hops(u, U_LOW_HOP, 1, lo, hi)
             step(u)
             at_slot(U_BACK, row_arrived, UP)
             at_slot(U_BACK, low_rank, 0, urecv, cot_of, 0, NZ)
@@ -500,8 +509,6 @@
             at_slot(U_LOW, row_arrived, DOWN)
             at_slot(U_LOW, low_rank, 1, drecv, tok_of, 0, NZ // 2)
             at_slot(U_LOW + 1, low_rank, 1, drecv, tok_of, NZ // 2, NZ)
-            hops(u, U_BACK_HOP, 0, lo, hi)
-            hops(u, U_LOW_HOP, 1, lo, hi)
             if lo < U_BASE + 2 * NC and U_BASE < hi:
                 every(u, U_BASE, 2, NC, base_chunk)
             at_slot(U_BACK_END, down_grads)
@@ -515,6 +522,8 @@
             at_slot(U_LOW_END, up_grads)
             at_slot(U_LOW_END + 1, send_grads, HGRAD, hgrads, hsend, hrecv)
             at_slot(U_LOW_END + 2, lora_values)
+            at_slot(U_SENT - 1, choose, 0)
+            at_slot(U_SENT + 1, choose, 1)
             at_slot(U_SENT, row_sent, TAG)
             at_slot(U_SENT, line_sent, UP)
             at_slot(U_SENT + 2, row_sent, UP)
@@ -583,7 +592,7 @@
         vm((2, NB, rh, HEAD), BF), vm((2, 8, 4, rh, HEAD), BF), vm((2, 8, 4, rh, HEAD), BF),
         vm((2, 4, OWN, rh, HEAD), BF), vm((2, 4, OWN, rh, HEAD), BF),
         vm((2, NZ, BLK, 2 * R), BF), vm((2, 2, 4, BLK, 2 * R), BF), vm((2, NZ, BLK, 2 * R), BF), vm((2, NZ, BLK, 2 * R), BF),
-        vm((ROWS, HEAD), BF),
+        vm((ROWS, HEAD), BF), vm((2, 4, OWN * rh, 8 * rh), BF),
         pltpu.SMEM((2, 8, 128), I32), pltpu.SMEM((8, 128), I32),
         dma((5,)),
         dma((2, MSG)), dma((2, MSG)), dma((2, MSG)), dma((2, MSG)),

time: 112 us -> 110 us (0.982)
  Pallas kernels: 110 us -> 108 us
    pallas_call x1, Pallas kernels: 108 us -> 106 us  [on_device(): pl.pallas_call(kernel, out_shape=(vm((ROWS, HEAD), BF), vm((ROWS, FEAT),...]
where the time goes in v5:
time: 110 us; the launch traced here: 109 us
  Pallas kernels  108 us (98%)
    pallas_call x1, Pallas kernels, on_device(): pl.pallas_call(kernel, out_shape=(vm((ROWS, HEAD), BF), vm((ROWS, FEAT),...  106 us

profile of v5, /device:TPU:6, one launch (start us, length us, event | category | flops | bytes accessed | tf_op | source)
XLA Modules:
  0.0 108.5 jit_solution(8560804502562826405)
XLA Ops:
  0.6 105.9 %shard_map.111 = (bf16[2048,128]{1,0:T(8,128)(2,1)S(1)}, bf16[2048,640]{1,0:T(8,128)(2,1)S(1)}, f32[4,64,640]{2,1,0:T(8,128)S(1)}, f32[4,64,128]{2,1,0:T(8,128)S(1)}) custom-call(s32[16]{0:T(128)} %ba_s.1, s32[128]{0:T(128)} %slot_s.1, s32[128]{0:T(128)} %rank_s.1, s32[1,128]{1,0:T(1,128)} %bitcast.5, s32[1,128]{1,0:T(1,128)} %bitcast.6, ...), custom_call_target="tpu_custom_call" | custom-call | tf_op jit(solution)/shard_map/pallas_call | solution.py:602
  106.6 1.9 %shard_map.112 = (bf16[2048,128]{1,0:T(8,128)(2,1)}, bf16[2048,640]{1,0:T(8,128)(2,1)}, f32[4,64,640]{2,1,0:T(8,128)}, f32[4,64,128]{2,1,0:T(8,128)}) custom-call(bf16[2048,128]{1,0:T(8,128)(2,1)S(1)} %get-tuple-element.12.refs_0_, bf16[2048,640]{1,0:T(8,128)(2,1)S(1)} %get-tuple-element.13.refs_1_, f32[4,64,640]{2,1,0:T(8,128)S(1)} %get-tuple-element.14.refs_2_, ...), custom_call_target="tpu_custom_call" | custom-call | tf_op jit(solution)/shard_map/pallas_call | solution.py:617
